TPU v7x, 512 devices: a whole 4x8x8 slice. The times are simulated.
512 devices in a mesh: ctx: 64 (over z, y), tp: 8 (over x, core).
Axes of the slice: x: 4, y: 8, z: 8, core: 2. Of those that a mesh axis runs over, the one named last changes fastest.
Arguments:
- queries: bfloat16 [2, 128, 128, 128], P(None, 'ctx', 'tp'), may hold values from -140 to 140
- key_codes: bfloat16 [8, 131072, 128], P('tp', 'ctx'), may hold values from -4.5 to 4.5
- key_scales: float32 [8, 131072], P('tp', 'ctx'), may hold values from 0.5 to 3
- value_codes: bfloat16 [8, 131072, 128], P('tp', 'ctx'), may hold values from -4 to 4
- value_scales: float32 [8, 131072], P('tp', 'ctx'), may hold values from 0.25 to 2
- lengths: int32 [128], replicated, may hold values from 65536 to 131072
- out_weight: bfloat16 [16384, 16384], P('tp', 'ctx'), may hold values from -0.046875 to 0.046875
Outputs:
- projected: bfloat16 [2, 128, 16384], P(None, 'tp', 'ctx')
All inputs are finite; a program needn't handle non-finite values.
Results may differ from a plain program's by a relative error of at most 0.023.
Values may be sent and summed in bfloat16 or wider, within the bound.
No kernel may reach another device: no remote copies, remote signals or barrier semaphores. Data moves between devices by JAX's collectives and lax.ppermute only.
A program may use at most 64 MiB of HBM per device.

v0:
```python
import math

import jax
import jax.numpy as jnp
from jax import lax
from jax.sharding import PartitionSpec as P


def hadamard_signs(order):
    position = jnp.arange(order, dtype=jnp.int32)
    common = jnp.bitwise_and(position[:, None], position[None, :])
    parity = jnp.zeros((order, order), jnp.int32)
    for shift_by in range(order.bit_length() - 1):
        parity = parity + jnp.bitwise_and(jnp.right_shift(common, shift_by), 1)
    return (1 - 2 * (parity % 2)).astype(jnp.float32)


def local(queries, key_codes, key_scales, value_codes, value_scales, lengths, out_weight):
    step_total, rows_own, heads_own, width = queries.shape
    group_total, memory_own = (key_codes.shape[0], key_codes.shape[1])
    per_group = heads_own // group_total
    inverse_square_root = 1.0 / math.sqrt(width)
    place = lax.axis_index("ctx")
    token = place * memory_own + jnp.arange(memory_own, dtype=jnp.int32)
    key_factor = key_scales * inverse_square_root
    piece = lax.all_gather(queries, "ctx", axis=1, tiled=True)
    row_count = piece.shape[1]
    block_rows = math.gcd(row_count, 16)
    block_count = row_count // block_rows
    query_blocks = jnp.moveaxis(
        piece.reshape(step_total, block_count, block_rows, group_total, per_group, width), 1, 0
    )
    limit_blocks = lengths.reshape(block_count, block_rows)

    def one_block(block_in):
        query_block, limit_block = block_in
        unscaled_logits = jnp.einsum(
            "srgpd,gmd->srgpm", query_block, key_codes, preferred_element_type=jnp.float32
        )
        score_logits = unscaled_logits * key_factor[None, None, :, None, :]
        valid = (token[None, :] < limit_block[:, None])[None, :, None, None, :]
        masked = jnp.where(valid, score_logits, -1e30)
        top = jnp.max(masked, axis=-1)
        expo = jnp.where(valid, jnp.exp(masked - top[..., None]), 0.0)
        total = jnp.sum(expo, axis=-1)
        weights = (expo * value_scales[None, None, :, None, :]).astype(jnp.bfloat16)
        summed = jnp.einsum(
            "srgpm,gmd->srgpd", weights, value_codes, preferred_element_type=jnp.float32
        )
        return (
            summed.reshape(step_total, block_rows, heads_own, width),
            top.reshape(step_total, block_rows, heads_own),
            total.reshape(step_total, block_rows, heads_own),
        )

    summed, top, total = lax.map(one_block, (query_blocks, limit_blocks))
    summed = jnp.moveaxis(summed, 0, 1).reshape(step_total, row_count, heads_own, width)
    top = jnp.moveaxis(top, 0, 1).reshape(step_total, row_count, heads_own)
    total = jnp.moveaxis(total, 0, 1).reshape(step_total, row_count, heads_own)
    summed, top, total = (summed, top, total)
    buffers = (summed, top, total)
    summed_buf, top_buf, total_buf = buffers
    peak = lax.pmax(top_buf, "ctx")
    factor = jnp.exp(top_buf - peak)
    scaled_sums = summed_buf * factor[..., None]
    scaled_totals = total_buf * factor
    pieces, piece_totals = (
        lax.all_to_all(
            scaled_sums[None].astype(jnp.bfloat16), "ctx", split_axis=2, concat_axis=0, tiled=True
        ).astype(jnp.float32),
        lax.all_to_all(
            scaled_totals[None].astype(jnp.bfloat16), "ctx", split_axis=2, concat_axis=0, tiled=True
        ).astype(jnp.float32),
    )
    numer = jnp.sum(pieces, axis=0)
    denom = jnp.sum(piece_totals, axis=0)
    rotated = (numer / denom[..., None]).reshape(step_total * rows_own * heads_own, width)
    signs = hadamard_signs(width)
    attended = (
        jnp.dot(rotated, signs, precision=lax.Precision.HIGHEST, preferred_element_type=jnp.float32)
        * inverse_square_root
    )
    attended = attended.astype(jnp.bfloat16).reshape(step_total, rows_own, heads_own * width)
    terms = jnp.einsum(
        "srk,kc->src",
        lax.all_gather(attended, "ctx", axis=1, tiled=True),
        out_weight,
        preferred_element_type=jnp.float32,
    )
    return lax.psum_scatter(terms.astype(jnp.bfloat16), "tp", scatter_dimension=1, tiled=True)


def solution(mesh):
    return jax.shard_map(
        local,
        mesh=mesh,
        in_specs=(
            P(None, "ctx", "tp", None),
            P("tp", "ctx", None),
            P("tp", "ctx"),
            P("tp", "ctx", None),
            P("tp", "ctx"),
            P(),
            P("tp", "ctx"),
        ),
        out_specs=P(None, "tp", "ctx"),
        check_vma=False,
    )
```

profile of v0, /device:TPU:1, one launch (start us, length us, event | category | flops | bytes accessed | tf_op | source)
XLA Modules:
  0.0 576.0 jit_solution(17793009666159267064)
XLA Ops:
  6.5 0.7 all-gather.3.cloned.1.call-update
  7.3 0.7 reshape.113
  8.0 0.7 broadcast_multiply_fusion
  8.7 82.3 %all-gather.3.cloned.1.call-done = bf16[2,128,16,128]{3,2,1,0:T(8,128)(2,1)} async-done(((bf16[2,2,16,128]{3,2,1,0:T(8,128)(2,1)}), bf16[2,128,16,128]{3,2,1,0:T(8,128)(2,1)}) %all-gather.3.cloned.1.call-update) | async-done | bytes 1048592 | tf_op jit(solution)/shard_map/all_gather | solution.py:26
  91.0 39.4 %while.15 = (s32[]{:T(128)}, f32[8,2,16,16,128]{4,3,2,0,1:T(8,128)S(1)}, f32[8,2,16,16]{3,2,1,0:T(8,128)S(1)}, f32[8,2,16,16]{3,2,1,0:T(8,128)S(1)}, s32[8,16]{1...) while((s32[]{:T(128)}, ...), condition=%wide.region_3.4_spmd.clone, body=%wide.region_0.3_spmd.clone.sunk | while | flops 551584768 | bytes 16423805 | solution.py:56
  91.1 2.0 fusion.61
  93.1 1.4 fusion.63
  94.6 1.4 fusion.62
  96.1 2.0 fusion.61
  98.1 1.4 fusion.63
  99.5 1.4 fusion.62
  101.0 2.0 fusion.61
  103.0 1.4 fusion.63
  104.4 1.4 fusion.62
  106.0 2.0 fusion.61
  108.0 1.4 fusion.63
  109.4 1.4 fusion.62
  110.9 2.0 fusion.61
  112.9 1.4 fusion.63
  114.3 1.4 fusion.62
  115.8 2.0 fusion.61
  117.8 1.4 fusion.63
  119.2 1.4 fusion.62
  120.8 2.0 fusion.61
  122.8 1.4 fusion.63
  124.2 1.4 fusion.62
  125.7 2.0 fusion.61
  127.7 1.4 fusion.63
  129.1 1.4 fusion.62
  130.5 0.1 copy.52
  130.6 0.1 reshape.116
  130.7 222.6 %pmax.7 = f32[2,128,16]{1,2,0:T(8,128)S(1)} all-reduce(f32[2,128,16]{1,2,0:T(8,128)S(1)} %reshape.116), channel_id=1, replica_groups=mesh['ctx'=64,'tp'=8] {'ctx'}, use_global_device_ids=true, to_apply=%region_4.5 | all-reduce | flops 4096 | bytes 32768 | tf_op jit(solution)/shard_map/pmax | solution.py:63
  353.3 0.1 copy.56
  353.6 0.1 copy.53
  353.7 0.7 copy.57
  354.4 5.5 all-to-all-start.1
  359.9 0.7 multiply_convert_fusion.1
  360.6 1.2 copy.54
  361.7 9.2 %all-to-all-done.1 = bf16[1,2,128,16]{3,1,0,2:T(2,128)(2,1)S(1)} async-done(((bf16[1,2,128,16]{3,1,0,2:T(2,128)(2,1)}), bf16[1,2,128,16]{3,1,0,2:T(2,128)(2,1)S(1)}, u32[]{:S(2)}, u32[]{:S(2)}) %all-to-all-start.1) | async-done | bytes 8224 | tf_op jit(solution)/shard_map/all_to_all | solution.py:71
  370.9 4.7 all-to-all-start
  375.7 0.1 copy.59
  376.0 18.5 %all-to-all-done = bf16[1,2,128,16,128]{4,3,1,0,2:T(8,128)(2,1)S(1)} async-done(((bf16[1,2,128,16,128]{4,3,1,0,2:T(8,128)(2,1)}), bf16[1,2,128,16,128]{4,3,1,0,2:T(8,128)(2,1)S(1)}, u32[]{:S(2)}, u32[]{:S(2)}) %all-to-all-start) | async-done | bytes 1048608 | tf_op jit(solution)/shard_map/all_to_all | solution.py:68
  394.5 0.2 convert_reduce_fusion
  394.8 0.3 fusion.25
  395.1 0.6 copy.60
  395.8 135.4 %all-gather.5.cloned.1.call-done = bf16[2,128,2048]{2,0,1:T(2,128)(2,1)} async-done(((bf16[2,2,2048]{2,0,1:T(2,128)(2,1)}), bf16[2,128,2048]{2,0,1:T(2,128)(2,1)}) %all-gather.5.cloned.1.call-update) | async-done | bytes 1048592 | tf_op jit(solution)/shard_map/all_gather | solution.py:86
  531.2 2.6 convolution_convert_fusion
  533.8 35.6 %reduce-scatter.2.cloned.1.call-done = bf16[2,16,256]{2,1,0:T(8,128)(2,1)} async-done(((bf16[2,128,256]{2,1,0:T(8,128)(2,1)}), bf16[2,16,256]{2,1,0:T(8,128)(2,1)}) %reduce-scatter.2.cloned.1.call-update) | async-done | bytes 16400 | tf_op jit(solution)/shard_map/reduce_scatter | solution.py:90
  (82 shorter events, 1.6 us)
Async XLA Ops:
  6.5 524.7 %copy-start = (bf16[2048,256]{1,0:T(8,128)(2,1)S(1)}, bf16[2048,256]{1,0:T(8,128)(2,1)}, u32[]{:S(2)}) copy-start(bf16[2048,256]{1,0:T(8,128)(2,1)} %param.15) | copy-start | bytes 3145732
  6.5 84.5 %all-gather.3.cloned.1.call-start = ((), (), s32[]{:S(2)}) async-start(), calls=%async_computation.3 | async-start | bytes 1064960 | tf_op jit(solution)/shard_map/all_gather | solution.py:26
  91.1 3.4 copy-start.1
  91.1 3.4 copy-start.2
  96.1 3.4 copy-start.1
  96.1 3.4 copy-start.2
  101.0 3.4 copy-start.1
  101.0 3.4 copy-start.2
  105.9 3.4 copy-start.1
  105.9 3.4 copy-start.2
  110.9 3.4 copy-start.1
  110.9 3.4 copy-start.2
  115.8 3.4 copy-start.1
  115.8 3.4 copy-start.2
  120.7 3.4 copy-start.1
  120.7 3.4 copy-start.2
  125.7 3.4 copy-start.1
  125.7 3.4 copy-start.2
  354.4 16.5 %all-to-all-start.1 = ((bf16[1,2,128,16]{3,1,0,2:T(2,128)(2,1)}), bf16[1,2,128,16]{3,1,0,2:T(2,128)(2,1)S(1)}, u32[]{:S(2)}, u32[]{:S(2)}) async-start(bf16[1,2,128,16]{3,1,0,2:T(2,128)(2,1)} %copy.57), calls=%async_computation.1 | async-start | bytes 131072 | tf_op jit(solution)/shard_map/all_to_all | solution.py:71
  370.9 23.6 %all-to-all-start = ((bf16[1,2,128,16,128]{4,3,1,0,2:T(8,128)(2,1)}), bf16[1,2,128,16,128]{4,3,1,0,2:T(8,128)(2,1)S(1)}, u32[]{:S(2)}, u32[]{:S(2)}) async-start(bf16[1,2,128,16,128]{4,3,1,0,2:T(8,128)(2,1)} %copy.54), calls=%async_computation | async-start | bytes 2097152 | tf_op jit(solution)/shard_map/all_to_all | solution.py:68
  375.6 155.6 %all-gather.5.cloned.1.call-start = ((), (), s32[]{:S(2)}) async-start(), calls=%async_computation.4 | async-start | bytes 1064960 | tf_op jit(solution)/shard_map/all_gather | solution.py:86
  395.7 173.7 %reduce-scatter.2.cloned.1.call-start = ((), (), s32[]{:S(2)}) async-start(), calls=%async_computation.5 | async-start | bytes 147456 | tf_op jit(solution)/shard_map/reduce_scatter | solution.py:90
Sparse Core Ops, SparseCore 0:
  10.3 80.6 all-gather.2
  395.9 135.2 all-gather.4
  534.0 35.3 reduce-scatter.1
where the time goes:
time: 577 us; the launch traced here: 576 us
  waiting for transfers between devices  282 us (49%)
  blocking collectives  223 us (39%)
  matrix products  29.7 us (5%)
  other arithmetic  13.5 us (2%)
  between operations  13.2 us (2%)
  starting transfers between devices  10.2 us (2%)
    pmax x1, blocking collectives, local(): peak = lax.pmax(top_buf, 'ctx')  223 us
    all_gather x1, waiting for transfers between devices, local(): lax.all_gather(attended, 'ctx', axis=1, tiled=True)  135 us
    all_gather x1, waiting for transfers between devices, local(): piece = lax.all_gather(queries, 'ctx', axis=1, tiled=True)  82.3 us
    reduce_scatter x1, waiting for transfers between devices, local(): lax.psum_scatter(terms.astype(jnp.bfloat16), 'tp', scatter_dimension=1, t...  35.6 us
    all_to_all x1, waiting for transfers between devices, local(): lax.all_to_all(scaled_sums[None].astype(jnp.bfloat16), 'ctx', split_axis=...  18.5 us
    dot_general x8, matrix products, one_block(): jnp.einsum('srgpd,gmd->srgpm', query_block, key_codes, preferred_element_...  16 us
  transfers between devices with their start and end apart: 5, of which 5 were waited for; matrix products, arithmetic and copies ran while one was open for 1% of the time, Pallas kernels for 0%

commit v1 on v0

v1 whole, which is shorter than its diff:
```python
import functools
import math

import jax
import jax.numpy as jnp
from jax import lax
from jax.experimental import pallas as pl
from jax.experimental.pallas import tpu as pltpu
from jax.sharding import PartitionSpec as P

F32 = jnp.float32
BF16 = jnp.bfloat16
LOG2E = 1.0 / math.log(2.0)
EXTRA = 8
NONE = -(2.0**100)


def split_two(x):
    high = x.astype(BF16).astype(F32)
    low = (x - high).astype(BF16).astype(F32)
    return high, low


def iota(shape, axis):
    return lax.broadcasted_iota(jnp.int32, shape, axis)


def attention_kernel(len_ref, q_ref, kt_ref, kf_ref, v_ref, out_ref, s_ref, p_ref, m_ref):
    sources, vectors, width = q_ref.shape
    tokens = kt_ref.shape[1]
    rows = sources * vectors
    group = pl.program_id(0)
    place = lax.axis_index("ctx")
    q = q_ref[...].reshape(rows, width)
    s_ref[...] = jnp.dot(q, kt_ref[...], preferred_element_type=F32)
    kf = kf_ref[...]
    token = place * tokens + iota((1, tokens), 1)
    sub = 16
    lane = iota((sub, width), 1)
    odd = iota((sub, 1), 0) % 2
    for at in range(0, rows, sub):
        own = group * (2 * sources) + 2 * (at // vectors)
        limit = jnp.where(odd == 0, len_ref[own], len_ref[own + 1])
        score = jnp.where(token < limit, s_ref[at : at + sub, :] * kf, NONE)
        high, low = split_two(jnp.max(score, axis=1, keepdims=True))
        p_ref[at : at + sub, :] = jnp.exp2(score - (high + low)).astype(BF16)
        m_ref[at : at + sub, :] = jnp.where(lane == 0, high, low)
    sums = jnp.dot(p_ref[...], v_ref[...], preferred_element_type=F32)
    high, low = split_two(sums[:, width:])
    lane = iota((rows, width), 1)
    extra = jnp.where(lane < 2, m_ref[...], jnp.where(lane == 2, high, low))
    pick = (iota((EXTRA, width), 0) == iota((EXTRA, width), 1)).astype(BF16)
    parts = vectors // 8
    pad = jnp.zeros((width - sources * 8, width), BF16)
    for part in range(parts):
        places = [source * vectors + part * 8 for source in range(sources)]
        block = jnp.concatenate([sums[at : at + 8, :width] for at in places], axis=0)
        out_ref[part, : sources * 8, :] = block.astype(BF16)
        block = jnp.concatenate([extra[at : at + 8, :] for at in places], axis=0).astype(BF16)
        block = jnp.concatenate([block, pad], axis=0)
        turned = lax.dot_general(pick, block, (((1,), (1,)), ((), ())), preferred_element_type=F32)
        out_ref[part, sources * 8 :, :] = turned.astype(BF16)


def combine_kernel(in_ref, out_ref):
    places, total_rows, width = in_ref.shape
    vectors = total_rows - EXTRA
    extra = in_ref[:, vectors:, :].astype(F32).reshape(places * EXTRA, width).astype(BF16)
    unit = (iota((vectors, width), 0) == iota((vectors, width), 1)).astype(BF16)
    turned = lax.dot_general(unit, extra, (((1,), (1,)), ((), ())), preferred_element_type=F32)
    turned = turned.astype(BF16)
    column = iota((places * EXTRA, places), 0)
    wanted = iota((places * EXTRA, places), 1) * EXTRA

    def kind(index):
        pick = (column == wanted + index).astype(BF16)
        return jnp.dot(turned, pick, preferred_element_type=F32)

    top = kind(0) + kind(1)
    total = kind(2) + kind(3)
    factor = jnp.exp2(top - jnp.max(top, axis=1, keepdims=True))
    denom = jnp.sum(factor * total, axis=1, keepdims=True)
    numer = jnp.zeros((vectors, width), F32)
    for at in range(places):
        numer = numer + factor[:, at : at + 1] * in_ref[at, :vectors, :].astype(F32)
    rotated = numer / denom
    common = iota((width, width), 0) & iota((width, width), 1)
    common = common ^ (common >> 4)
    common = common ^ (common >> 2)
    common = common ^ (common >> 1)
    signs = (1 - 2 * (common & 1)).astype(F32)
    attended = jnp.dot(rotated, signs, precision=lax.Precision.HIGHEST, preferred_element_type=F32)
    attended = (attended * (1.0 / math.sqrt(width))).astype(BF16)
    new = iota((vectors, vectors), 0)
    old = iota((vectors, vectors), 1)
    source = (new % 16) // 2
    pick = (old == source * 8 + (new // 16) * 2 + new % 2).astype(BF16)
    attended = jnp.dot(pick, attended, preferred_element_type=F32).astype(BF16)
    for at in range(places):
        out_ref[at] = attended


def project_kernel(in_ref, w_ref, out_ref):
    groups, pairs, vectors, width = in_ref.shape
    half = vectors // 2
    terms = jnp.zeros((groups * half, w_ref.shape[1]), F32)
    for pair in range(pairs):
        both = [
            in_ref[:, pair, at : at + half, :].reshape(groups * half, width) for at in (0, half)
        ]
        terms = terms + jnp.dot(
            jnp.concatenate(both, axis=1),
            w_ref[pair * 2 * width : (pair + 1) * 2 * width, :],
            preferred_element_type=F32,
        )
    out_ref[...] = terms.astype(BF16).reshape(out_ref.shape)


def local(queries, key_codes, key_scales, value_codes, value_scales, lengths, out_weight):
    steps, rows_own, heads, width = queries.shape
    tokens = key_codes.shape[1]
    places = lax.axis_size("ctx")
    groups = lax.axis_size("tp")
    sources = places // groups
    vectors = steps * rows_own * heads

    own = queries.transpose(2, 0, 1, 3).reshape(1, vectors, width)
    query = lax.all_to_all(
        jnp.broadcast_to(own, (places, vectors, width)), "ctx", 0, 0, tiled=True
    )
    key_turned = key_codes[0].T
    key_factor = key_scales * (LOG2E / math.sqrt(width))
    value = (value_codes[0].astype(F32) * value_scales[0][:, None]).astype(BF16)
    value = jnp.concatenate([value, jnp.ones_like(value)], axis=1)

    block = sources * vectors
    whole = lambda *shape: pl.BlockSpec(shape, lambda i: (0,) * len(shape))
    partial = pl.pallas_call(
        attention_kernel,
        grid=(groups,),
        out_shape=jax.ShapeDtypeStruct((places, vectors + EXTRA, width), BF16),
        in_specs=[
            pl.BlockSpec(memory_space=pltpu.SMEM),
            pl.BlockSpec((sources, vectors, width), lambda i: (i, 0, 0)),
            whole(width, tokens),
            whole(1, tokens),
            whole(tokens, 2 * width),
        ],
        out_specs=pl.BlockSpec((sources, vectors + EXTRA, width), lambda i: (i, 0, 0)),
        scratch_shapes=[
            pltpu.VMEM((block, tokens), F32),
            pltpu.VMEM((block, tokens), BF16),
            pltpu.VMEM((block, width), F32),
        ],
        compiler_params=pltpu.CompilerParams(vmem_limit_bytes=48 * 1024 * 1024),
        cost_estimate=pl.CostEstimate(
            flops=8 * places * vectors * tokens * width,
            bytes_accessed=8 * 1024 * 1024,
            transcendentals=places * vectors * tokens,
        ),
        name="attention",
    )(lengths, query, key_turned, key_factor, value)

    pieces = lax.all_to_all(partial, "ctx", 0, 0, tiled=True)
    params = pltpu.CompilerParams(vmem_limit_bytes=32 * 1024 * 1024)
    attended = pl.pallas_call(
        combine_kernel,
        out_shape=jax.ShapeDtypeStruct((places, vectors, width), BF16),
        compiler_params=params,
        name="combine",
    )(pieces)
    attended = lax.all_to_all(attended, "ctx", 0, 0, tiled=True)
    half = vectors // 2
    terms = pl.pallas_call(
        project_kernel,
        out_shape=jax.ShapeDtypeStruct((groups, half, out_weight.shape[1]), BF16),
        compiler_params=params,
        name="project",
    )(attended.reshape(groups, sources, vectors, width), out_weight)
    terms = lax.all_to_all(terms, "tp", 0, 0, tiled=True)
    projected = jnp.sum(terms.astype(F32), axis=0).astype(BF16)
    return projected.reshape(steps, half // steps, out_weight.shape[1])


def solution(mesh):
    return jax.shard_map(
        local,
        mesh=mesh,
        in_specs=(
            P(None, "ctx", "tp", None),
            P("tp", "ctx", None),
            P("tp", "ctx"),
            P("tp", "ctx", None),
            P("tp", "ctx"),
            P(),
            P("tp", "ctx"),
        ),
        out_specs=P(None, "tp", "ctx"),
        check_vma=False,
    )
```

time: 577 us -> 157 us (0.27)
  waiting for transfers between devices: 282 us -> 26.5 us
  blocking collectives: 223 us -> 84.5 us
  matrix products: 29.7 us -> 0 us
  Pallas kernels: 0 us -> 24.6 us
  between operations: 13.2 us -> 0.1 us
  other arithmetic: 13.5 us -> 0.97 us
  starting transfers between devices: 10.2 us -> 17.3 us
    pmax x1 -> x0, blocking collectives: 223 us -> none  [local(): peak = lax.pmax(top_buf, 'ctx')]
    all_gather x2 -> x0, waiting for transfers between devices: 218 us -> none  [the longest x1 135 us: local(): lax.all_gather(attended, 'ctx', axis=1, tiled=True)]
    all_to_all x0 -> x3, blocking collectives: none -> 84.5 us  [the longest x1 36 us: local(): pieces = lax.all_to_all(partial, 'ctx', 0, 0, tiled=True)]
    reduce_scatter x1 -> x0, waiting for transfers between devices: 35.6 us -> none  [local(): lax.psum_scatter(terms.astype(jnp.bfloat16), 'tp', scatter_dimension=1, t...]
    dot_general x18 -> x0, matrix products: 29.7 us -> none  [the longest x8 16 us: one_block(): jnp.einsum('srgpd,gmd->srgpm', query_block, key_codes, preferred_element_...]
    pallas_call x0 -> x3, Pallas kernels: none -> 24.6 us  [the longest x1 22.3 us: local(): pl.pallas_call(attention_kernel, grid=(groups,), out_shape=jax.ShapeDtype...]
    reduce_sum x10 -> x1, other arithmetic: 11.2 us -> 0.63 us  [local(): projected = jnp.sum(terms.astype(F32), axis=0).astype(BF16)]
    all_to_all x2 -> x1, starting transfers between devices: 10.1 us -> 17.3 us  [local(): lax.all_to_all(jnp.broadcast_to(own, (places, vectors, width)), 'ctx', 0,...]
  transfers between devices with their start and end apart: 5 -> 1, of which waited for: 5 -> 1; matrix products, arithmetic and copies ran while one was open for 1% -> 0% of each run, Pallas kernels for 0% -> 0%
where the time goes in v1:
time: 157 us; the launch traced here: 156 us
  blocking collectives  84.5 us (54%)
  waiting for transfers between devices  26.5 us (17%)
  Pallas kernels  24.6 us (16%)
  starting transfers between devices  17.3 us (11%)
  local copies, waits for them, and re-layouts  2.53 us (2%)
    all_to_all x1, blocking collectives, local(): pieces = lax.all_to_all(partial, 'ctx', 0, 0, tiled=True)  36 us
    all_to_all x1, blocking collectives, local(): attended = lax.all_to_all(attended, 'ctx', 0, 0, tiled=True)  34.5 us
    all_to_all x1, waiting for transfers between devices, local(): lax.all_to_all(jnp.broadcast_to(own, (places, vectors, width)), 'ctx', 0,...  26.5 us
    pallas_call x1, Pallas kernels, local(): pl.pallas_call(attention_kernel, grid=(groups,), out_shape=jax.ShapeDtype...  22.3 us
    all_to_all x1, starting transfers between devices, local(): lax.all_to_all(jnp.broadcast_to(own, (places, vectors, width)), 'ctx', 0,...  17.3 us
    all_to_all x1, blocking collectives, local(): terms = lax.all_to_all(terms, 'tp', 0, 0, tiled=True)  14 us
  transfers between devices with their start and end apart: 1, of which 1 were waited for; matrix products, arithmetic and copies ran while one was open for 0% of the time, Pallas kernels for 0%

profile of v1, /device:TPU:1, one launch (start us, length us, event | category | flops | bytes accessed | tf_op | source)
XLA Modules:
  0.0 156.4 jit_solution(3884122374370042877)
XLA Ops:
  0.0 0.7 copy.9
  0.7 1.2 broadcast_in_dim.9
  2.0 0.0 copy-start.2
  2.0 0.0 copy-start.3
  2.0 0.0 copy-start.4
  2.0 17.3 %all-to-all-start = ((bf16[64,64,128]{2,1,0:T(8,128)(2,1)}), bf16[64,64,128]{2,1,0:T(8,128)(2,1)S(1)}, u32[]{:S(2)}, u32[]{:S(2)}) async-start(bf16[64,64,128]{2,1,0:T(8,128)(2,1)} %broadcast_in_dim.9), calls=%async_computation | async-start | bytes 2097152 | tf_op jit(solution)/shard_map/all_to_all | solution.py:128
  19.2 0.0 copy-done.2
  19.3 0.2 copy.10
  19.5 0.0 copy-done.3
  19.5 0.0 copy-done.4
  19.5 0.0 copy-start.5
  19.5 0.0 copy-start.1
  19.5 0.3 fusion
  19.9 0.1 concatenate.3.v_ref
  20.0 0.2 copy-done.5
  20.2 26.5 %all-to-all-done.q_ref = bf16[64,64,128]{2,1,0:T(8,128)(2,1)S(1)} async-done(((bf16[64,64,128]{2,1,0:T(8,128)(2,1)}), bf16[64,64,128]{2,1,0:T(8,128)(2,1)S(1)}, u32[]{:S(2)}, u32[]{:S(2)}) %all-to-all-start) | async-done | bytes 1048608 | tf_op jit(solution)/shard_map/all_to_all | solution.py:128
  46.7 0.0 copy-done.1
  46.7 22.3 %attention.1 = bf16[64,72,128]{2,1,0:T(8,128)(2,1)S(1)} custom-call(s32[128]{0:T(128)S(1)} %copy-done.1, bf16[64,64,128]{2,1,0:T(8,128)(2,1)S(1)} %all-to-all-done.q_ref, bf16[128,2048]{1,0:T(8,128)(2,1)S(1)} %bitcast.12, f32[1,2048]{1,0:T(1,128)S(1)} %broadcast_multiply_fusion.kf_ref, bf16[2048,256]{1,0:T(8,128)(2,1)S(1)} %concatenate.3.v_ref), custom_call_target="tpu_custom_call" | custom-call | flops 8589934592 | bytes 8388608 | tf_op jit(solution)/shard_map/attention/pallas_call | solution.py:138
  69.0 36.0 %all_to_all.20.in_ref = bf16[64,72,128]{2,1,0:T(8,128)(2,1)S(1)} all-to-all(bf16[64,72,128]{2,1,0:T(8,128)(2,1)S(1)} %attention.1), channel_id=1, replica_groups=mesh['ctx'=64,'tp'=8] {'ctx'}, dimensions={0} | all-to-all | bytes 2359296 | tf_op jit(solution)/shard_map/all_to_all | solution.py:164
  105.0 1.8 %combine.1 = bf16[64,64,128]{2,1,0:T(8,128)(2,1)S(1)} custom-call(bf16[64,72,128]{2,1,0:T(8,128)(2,1)S(1)} %all_to_all.20.in_ref), custom_call_target="tpu_custom_call" | custom-call | tf_op jit(solution)/shard_map/combine/pallas_call | solution.py:166
  106.8 0.0 copy-start
  106.9 34.5 %all_to_all.21 = bf16[64,64,128]{2,1,0:T(8,128)(2,1)S(1)} all-to-all(bf16[64,64,128]{2,1,0:T(8,128)(2,1)S(1)} %combine.1), channel_id=1, replica_groups=mesh['ctx'=64,'tp'=8] {'ctx'}, dimensions={0} | all-to-all | bytes 2097152 | tf_op jit(solution)/shard_map/all_to_all | solution.py:172
  141.3 0.0 copy-done
  141.3 0.4 project.1
  141.8 14.0 %all_to_all.22 = bf16[8,32,256]{2,1,0:T(8,128)(2,1)S(1)} all-to-all(bf16[8,32,256]{2,1,0:T(8,128)(2,1)S(1)} %project.1), channel_id=1, replica_groups=mesh['ctx'=64,'tp'=8] {'tp'}, dimensions={0} | all-to-all | bytes 262144 | tf_op jit(solution)/shard_map/all_to_all | solution.py:180
  155.8 0.6 reduce_sum.12
  (1 shorter events, 0.0 us)
Async XLA Ops:
  2.0 17.3 %copy-start.2 = (bf16[1,2048,128]{2,1,0:T(8,128)(2,1)S(1)}, bf16[1,2048,128]{2,1,0:T(8,128)(2,1)}, u32[]{:S(2)}) copy-start(bf16[1,2048,128]{2,1,0:T(8,128)(2,1)} %param.8) | copy-start | bytes 1572868
  2.0 17.5 %copy-start.3 = (bf16[1,2048,128]{2,1,0:T(8,128)(2,1)S(1)}, bf16[1,2048,128]{2,1,0:T(8,128)(2,1)}, u32[]{:S(2)}) copy-start(bf16[1,2048,128]{2,1,0:T(8,128)(2,1)} %param.10) | copy-start | bytes 1572868
  2.0 17.5 %copy-start.4 = (f32[1,2048]{1,0:T(1,128)S(1)}, f32[1,2048]{1,0:T(1,128)}, u32[]{:S(2)}) copy-start(f32[1,2048]{1,0:T(1,128)} %param.11) | copy-start | bytes 24580
  2.0 44.7 %all-to-all-start = ((bf16[64,64,128]{2,1,0:T(8,128)(2,1)}), bf16[64,64,128]{2,1,0:T(8,128)(2,1)S(1)}, u32[]{:S(2)}, u32[]{:S(2)}) async-start(bf16[64,64,128]{2,1,0:T(8,128)(2,1)} %broadcast_in_dim.9), calls=%async_computation | async-start | bytes 2097152 | tf_op jit(solution)/shard_map/all_to_all | solution.py:128
  19.5 0.7 copy-start.5
  19.5 27.2 %copy-start.1 = (s32[128]{0:T(128)S(1)}, s32[128]{0:T(128)}, u32[]{:S(2)}) copy-start(s32[128]{0:T(128)} %len_ref.1) | copy-start | bytes 1540
  106.8 34.5 %copy-start = (bf16[2048,256]{1,0:T(8,128)(2,1)S(1)}, bf16[2048,256]{1,0:T(8,128)(2,1)}, u32[]{:S(2)}) copy-start(bf16[2048,256]{1,0:T(8,128)(2,1)} %w_ref.1) | copy-start | bytes 3145732

commit v2 on v1

--- a/solution.py
+++ b/solution.py
@@ -25,41 +25,93 @@
     return lax.broadcasted_iota(jnp.int32, shape, axis)
 
 
-def attention_kernel(len_ref, q_ref, kt_ref, kf_ref, v_ref, out_ref, s_ref, p_ref, m_ref):
-    sources, vectors, width = q_ref.shape
+def attention_kernel(
+    len_ref, q_ref, kt_ref, kf_ref, v_ref, out_ref, s_even, s_odd, p_even, p_odd, m_even, m_odd
+):
+    vectors, width = q_ref.shape[1:]
     tokens = kt_ref.shape[1]
-    rows = sources * vectors
-    group = pl.program_id(0)
-    place = lax.axis_index("ctx")
-    q = q_ref[...].reshape(rows, width)
-    s_ref[...] = jnp.dot(q, kt_ref[...], preferred_element_type=F32)
-    kf = kf_ref[...]
-    token = place * tokens + iota((1, tokens), 1)
+    rows = s_even.shape[0]
+    sources = rows // vectors
+    groups = q_ref.shape[0] // sources
+    parts = vectors // 8
     sub = 16
-    lane = iota((sub, width), 1)
-    odd = iota((sub, 1), 0) % 2
-    for at in range(0, rows, sub):
-        own = group * (2 * sources) + 2 * (at // vectors)
-        limit = jnp.where(odd == 0, len_ref[own], len_ref[own + 1])
-        score = jnp.where(token < limit, s_ref[at : at + sub, :] * kf, NONE)
-        high, low = split_two(jnp.max(score, axis=1, keepdims=True))
-        p_ref[at : at + sub, :] = jnp.exp2(score - (high + low)).astype(BF16)
-        m_ref[at : at + sub, :] = jnp.where(lane == 0, high, low)
-    sums = jnp.dot(p_ref[...], v_ref[...], preferred_element_type=F32)
-    high, low = split_two(sums[:, width:])
-    lane = iota((rows, width), 1)
-    extra = jnp.where(lane < 2, m_ref[...], jnp.where(lane == 2, high, low))
-    pick = (iota((EXTRA, width), 0) == iota((EXTRA, width), 1)).astype(BF16)
-    parts = vectors // 8
-    pad = jnp.zeros((width - sources * 8, width), BF16)
-    for part in range(parts):
-        places = [source * vectors + part * 8 for source in range(sources)]
-        block = jnp.concatenate([sums[at : at + 8, :width] for at in places], axis=0)
-        out_ref[part, : sources * 8, :] = block.astype(BF16)
-        block = jnp.concatenate([extra[at : at + 8, :] for at in places], axis=0).astype(BF16)
-        block = jnp.concatenate([block, pad], axis=0)
-        turned = lax.dot_general(pick, block, (((1,), (1,)), ((), ())), preferred_element_type=F32)
-        out_ref[part, sources * 8 :, :] = turned.astype(BF16)
+    start = lax.axis_index("ctx") * tokens
+    scores, weights, marks = (s_even, s_odd), (p_even, p_odd), (m_even, m_odd)
+
+    def limits(group, source):
+        row = (group * sources + source) * 2
+        return len_ref[row] - start, len_ref[row + 1] - start
+
+    def score(group, slot):
+        q = q_ref[pl.ds(group * sources, sources)].reshape(rows, width)
+        scores[slot][...] = jnp.dot(q, kt_ref[...], preferred_element_type=F32)
+
+    def mask(group, slot):
+        for source in range(sources):
+            even, odd = limits(group, source)
+            inside = ((even > 0) & (even < tokens)) | ((odd > 0) & (odd < tokens))
+
+            @pl.when(inside)
+            def _():
+                first = jnp.where(even <= 0, tokens, even)
+                second = jnp.where(odd <= 0, tokens, odd)
+                limit = jnp.where(iota((sub, 1), 0) % 2 == 0, first, second)
+                valid = iota((1, tokens), 1) < limit
+                for at in range(source * vectors, (source + 1) * vectors, sub):
+                    held = scores[slot][at : at + sub, :]
+                    scores[slot][at : at + sub, :] = jnp.where(valid, held, NONE)
+
+    def weigh(group, slot):
+        kf = kf_ref[...]
+        lane = iota((sub, width), 1)
+        for at in range(0, rows, sub):
+            even, odd = limits(group, at // vectors)
+            some = jnp.where(iota((sub, 1), 0) % 2 == 0, even, odd) > 0
+            scaled = scores[slot][at : at + sub, :] * kf
+            high, low = split_two(jnp.max(scaled, axis=1, keepdims=True))
+            weights[slot][at : at + sub, :] = jnp.exp2(scaled - (high + low)).astype(BF16)
+            high = jnp.where(some, high, NONE)
+            low = jnp.where(some, low, 0.0)
+            marks[slot][at : at + sub, :] = jnp.where(lane == 0, high, low)
+
+    def gather(group, slot):
+        sums = jnp.dot(weights[slot][...], v_ref[...], preferred_element_type=F32)
+        high, low = split_two(sums[:, width:])
+        lane = iota((rows, width), 1)
+        extra = jnp.where(lane < 2, marks[slot][...], jnp.where(lane == 2, high, low))
+        extras = []
+        for part in range(parts):
+            places = [source * vectors + part * 8 for source in range(sources)]
+            block = jnp.concatenate([sums[at : at + 8, :width] for at in places], axis=0)
+            out_ref[group * parts + part, :vectors, :] = block.astype(BF16)
+            extras += [extra[at : at + 8, :] for at in places]
+        extras = jnp.concatenate(extras, axis=0).astype(BF16)
+        pick = (iota((EXTRA, width), 0) == iota((EXTRA, width), 1)).astype(BF16)
+        turned = lax.dot_general(pick, extras, (((1,), (1,)), ((), ())), preferred_element_type=F32)
+        for part in range(parts):
+            at = part // 2 * width
+            row = turned[:, at : at + width]
+            if part % 2:
+                row = pltpu.roll(row, vectors, 1)
+            out_ref[group * parts + part, vectors:, :] = row.astype(BF16)
+
+    def step(group, slot):
+        mask(group - 1, 1 - slot)
+        score(group, slot)
+        weigh(group - 1, 1 - slot)
+        gather(group - 1, 1 - slot)
+
+    def pair(index, carry):
+        step(2 * index, 0)
+        step(2 * index + 1, 1)
+        return carry
+
+    score(0, 0)
+    step(1, 1)
+    lax.fori_loop(1, groups // 2, pair, 0)
+    mask(groups - 1, 1)
+    weigh(groups - 1, 1)
+    gather(groups - 1, 1)
 
 
 def combine_kernel(in_ref, out_ref):
@@ -125,33 +177,50 @@
     vectors = steps * rows_own * heads
 
     own = queries.transpose(2, 0, 1, 3).reshape(1, vectors, width)
-    query = lax.all_to_all(
-        jnp.broadcast_to(own, (places, vectors, width)), "ctx", 0, 0, tiled=True
+
+    def direct(own):
+        return lax.all_to_all(
+            jnp.broadcast_to(own, (places, vectors, width)), "ctx", 0, 0, tiled=True
+        )
+
+    def two_stages(own):
+        lines = [[at * sources + i for i in range(sources)] for at in range(groups)]
+        across = [[i * sources + at for i in range(groups)] for at in range(sources)]
+        line = lax.all_to_all(
+            jnp.broadcast_to(own, (sources, vectors, width)),
+            "ctx", 0, 0, axis_index_groups=lines, tiled=True,
+        )
+        line = line.reshape(1, sources * vectors, width)
+        whole = lax.all_to_all(
+            jnp.broadcast_to(line, (groups, sources * vectors, width)),
+            "ctx", 0, 0, axis_index_groups=across, tiled=True,
+        )
+        return whole.reshape(places, vectors, width)
+
+    def prepare(key_codes, key_scales, value_codes, value_scales):
+        value = (value_codes[0].astype(F32) * value_scales[0][:, None]).astype(BF16)
+        value = jnp.concatenate([value, jnp.ones_like(value)], axis=1)
+        return key_codes[0].T, key_scales * (LOG2E / math.sqrt(width)), value
+
+    memory = (key_codes, key_scales, value_codes, value_scales)
+    query, (key_turned, key_factor, value) = lax.cond(
+        lax.axis_index("tp") % 2 == 0,
+        lambda own, memory: (direct(own), prepare(*memory)),
+        lambda own, memory: (two_stages(own), prepare(*memory)),
+        own,
+        memory,
     )
-    key_turned = key_codes[0].T
-    key_factor = key_scales * (LOG2E / math.sqrt(width))
-    value = (value_codes[0].astype(F32) * value_scales[0][:, None]).astype(BF16)
-    value = jnp.concatenate([value, jnp.ones_like(value)], axis=1)
 
     block = sources * vectors
-    whole = lambda *shape: pl.BlockSpec(shape, lambda i: (0,) * len(shape))
+    vmem = pl.BlockSpec(memory_space=pltpu.VMEM)
     partial = pl.pallas_call(
         attention_kernel,
-        grid=(groups,),
         out_shape=jax.ShapeDtypeStruct((places, vectors + EXTRA, width), BF16),
-        in_specs=[
-            pl.BlockSpec(memory_space=pltpu.SMEM),
-            pl.BlockSpec((sources, vectors, width), lambda i: (i, 0, 0)),
-            whole(width, tokens),
-            whole(1, tokens),
-            whole(tokens, 2 * width),
-        ],
-        out_specs=pl.BlockSpec((sources, vectors + EXTRA, width), lambda i: (i, 0, 0)),
-        scratch_shapes=[
-            pltpu.VMEM((block, tokens), F32),
-            pltpu.VMEM((block, tokens), BF16),
-            pltpu.VMEM((block, width), F32),
-        ],
+        in_specs=[pl.BlockSpec(memory_space=pltpu.SMEM), vmem, vmem, vmem, vmem],
+        out_specs=vmem,
+        scratch_shapes=[pltpu.VMEM((block, tokens), F32)] * 2
+        + [pltpu.VMEM((block, tokens), BF16)] * 2
+        + [pltpu.VMEM((block, width), F32)] * 2,
         compiler_params=pltpu.CompilerParams(vmem_limit_bytes=48 * 1024 * 1024),
         cost_estimate=pl.CostEstimate(
             flops=8 * places * vectors * tokens * width,

time: 157 us -> 144 us (0.917)
  starting transfers between devices: 17.3 us -> 10.2 us
  Pallas kernels: 24.6 us -> 19.6 us
  waiting for transfers between devices: 26.5 us -> 22.3 us
  blocking collectives: 84.5 us -> 87.8 us
    all_to_all x0 -> x1, blocking collectives: none -> 15.4 us  [two_stages(): lax.all_to_all(jnp.broadcast_to(own, (sources, vectors, width)), 'ctx', 0...]
    all_to_all x1, starting transfers between devices: 17.3 us -> 10.2 us  [two_stages(): lax.all_to_all(jnp.broadcast_to(line, (groups, sources * vectors, width))...]
    pallas_call x1, Pallas kernels: 22.3 us -> 17.3 us  [local(): pl.pallas_call(attention_kernel, out_shape=jax.ShapeDtypeStruct((places,...]
    all_to_all x1, blocking collectives: 14 us -> 9.49 us  [local(): terms = lax.all_to_all(terms, 'tp', 0, 0, tiled=True)]
    all_to_all x1, blocking collectives: 36 us -> 31.6 us  [local(): pieces = lax.all_to_all(partial, 'ctx', 0, 0, tiled=True)]
    all_to_all x1, waiting for transfers between devices: 26.5 us -> 22.3 us  [two_stages(): lax.all_to_all(jnp.broadcast_to(line, (groups, sources * vectors, width))...]
    all_to_all x1, blocking collectives: 34.5 us -> 31.3 us  [local(): attended = lax.all_to_all(attended, 'ctx', 0, 0, tiled=True)]
where the time goes in v2:
time: 144 us; the launch traced here: 143 us
  blocking collectives  87.8 us (61%)
  waiting for transfers between devices  22.3 us (15%)
  Pallas kernels  19.6 us (14%)
  starting transfers between devices  10.2 us (7%)
  local copies, waits for them, and re-layouts  2.48 us (2%)
    all_to_all x1, blocking collectives, local(): pieces = lax.all_to_all(partial, 'ctx', 0, 0, tiled=True)  31.6 us
    all_to_all x1, blocking collectives, local(): attended = lax.all_to_all(attended, 'ctx', 0, 0, tiled=True)  31.3 us
    all_to_all x1, waiting for transfers between devices, two_stages(): lax.all_to_all(jnp.broadcast_to(line, (groups, sources * vectors, width))...  22.3 us
    pallas_call x1, Pallas kernels, local(): pl.pallas_call(attention_kernel, out_shape=jax.ShapeDtypeStruct((places,...  17.3 us
    all_to_all x1, blocking collectives, two_stages(): lax.all_to_all(jnp.broadcast_to(own, (sources, vectors, width)), 'ctx', 0...  15.4 us
    all_to_all x1, starting transfers between devices, two_stages(): lax.all_to_all(jnp.broadcast_to(line, (groups, sources * vectors, width))...  10.2 us
    all_to_all x1, blocking collectives, local(): terms = lax.all_to_all(terms, 'tp', 0, 0, tiled=True)  9.49 us
  transfers between devices with their start and end apart: 1, of which 1 were waited for; matrix products, arithmetic and copies ran while one was open for 0% of the time, Pallas kernels for 0%

profile of v2, /device:TPU:1, one launch (start us, length us, event | category | flops | bytes accessed | tf_op | source)
XLA Modules:
  0.0 143.4 jit_solution(796842166492415633)
XLA Ops:
  0.0 0.0 copy-start.1
  0.0 50.7 %conditional.1 = (bf16[64,64,128]{2,1,0:T(8,128)(2,1)}, f32[1,2048]{1,0:T(1,128)S(1)}, bf16[2048,256]{1,0:T(8,128)(2,1)S(1)}, bf16[128,2048]{1,0:T(8,128)(2,1)S(1)}) conditional(s32[]{:T(128)} %convert_element_type.23, (bf16[16,2,2,128]{3,0,2,1:T(8,128)(2,1)}, bf16[1,2048,128]{2,1,0:T(8,128)(2,1)}, f32[1,2048]{1,0:T(1,128)}, ...), branch_computations={%region_0.1_spmd, %region_1.2_spmd} | conditional | flops 788480 | bytes 12722354 | solution.py:206
  0.0 0.7 copy.12
  0.8 15.4 %all_to_all.27 = bf16[8,64,128]{2,1,0:T(8,128)(2,1)S(1)} all-to-all(bf16[8,64,128]{2,1,0:T(8,128)(2,1)S(1)} %broadcast_in_dim.13), channel_id=1, replica_groups={{0,8,16,24,32,40,48,56},{64,72,80,88,96,104,112,120},{128,136,144,152,1..., dimensions={0} | all-to-all | bytes 262144 | tf_op jit(solution)/shard_map/cond/branch_0_fun/all_to_all | solution.py:189
  16.2 1.1 broadcast_in_dim.18
  17.3 0.0 copy-start.2
  17.3 0.0 copy-start.4
  17.3 0.0 copy-start.6
  17.3 10.2 %all-to-all-start.1 = ((bf16[8,512,128]{2,1,0:T(8,128)(2,1)}), bf16[8,512,128]{2,1,0:T(8,128)(2,1)}, u32[]{:S(2)}, u32[]{:S(2)}) async-start(bf16[8,512,128]{2,1,0:T(8,128)(2,1)} %broadcast_in_dim.18), calls=%async_computation.1 | async-start | bytes 2097152 | tf_op jit(solution)/shard_map/cond/branch_0_fun/all_to_all | solution.py:194
  27.5 0.0 copy-done.2
  27.5 0.2 copy.10
  27.7 0.0 copy-done.4
  27.7 0.0 copy-done.6
  27.7 0.0 copy-start.8
  27.7 0.3 fusion
  28.1 0.1 concatenate.4
  28.2 0.2 copy-done.8
  28.4 22.3 %all-to-all-done.1 = bf16[8,512,128]{2,1,0:T(8,128)(2,1)} async-done(((bf16[8,512,128]{2,1,0:T(8,128)(2,1)}), bf16[8,512,128]{2,1,0:T(8,128)(2,1)}, u32[]{:S(2)}, u32[]{:S(2)}) %all-to-all-start.1) | async-done | bytes 1048608 | tf_op jit(solution)/shard_map/cond/branch_0_fun/all_to_all | solution.py:194
  50.7 0.0 copy-done.1
  50.7 17.3 %attention.1 = bf16[64,72,128]{2,1,0:T(8,128)(2,1)S(1)} custom-call(s32[128]{0:T(128)S(1)} %copy-done.1, bf16[64,64,128]{2,1,0:T(8,128)(2,1)} %get-tuple-element.39.q_ref, bf16[128,2048]{1,0:T(8,128)(2,1)S(1)} %get-tuple-element.43.kt_ref, f32[1,2048]{1,0:T(1,128)S(1)} %get-tuple-element.41.kf_ref, bf16[2048,256]{1,0:T(8,128)(2,1)S(1)} %get-tuple-element.42.v_ref), custom_call_target="tpu_custom_call" | custom-call | flops 8589934592 | bytes 8388608 | tf_op jit(solution)/shard_map/attention/pallas_call | solution.py:216
  68.0 31.6 %all_to_all.28.in_ref = bf16[64,72,128]{2,1,0:T(8,128)(2,1)S(1)} all-to-all(bf16[64,72,128]{2,1,0:T(8,128)(2,1)S(1)} %attention.1), channel_id=1, replica_groups=mesh['ctx'=64,'tp'=8] {'ctx'}, dimensions={0} | all-to-all | bytes 2359296 | tf_op jit(solution)/shard_map/all_to_all | solution.py:233
  99.6 1.8 %combine.1 = bf16[64,64,128]{2,1,0:T(8,128)(2,1)S(1)} custom-call(bf16[64,72,128]{2,1,0:T(8,128)(2,1)S(1)} %all_to_all.28.in_ref), custom_call_target="tpu_custom_call" | custom-call | tf_op jit(solution)/shard_map/combine/pallas_call | solution.py:235
  101.5 0.0 copy-start
  101.5 31.3 %all_to_all.29 = bf16[64,64,128]{2,1,0:T(8,128)(2,1)S(1)} all-to-all(bf16[64,64,128]{2,1,0:T(8,128)(2,1)S(1)} %combine.1), channel_id=1, replica_groups=mesh['ctx'=64,'tp'=8] {'ctx'}, dimensions={0} | all-to-all | bytes 2097152 | tf_op jit(solution)/shard_map/all_to_all | solution.py:241
  132.8 0.0 copy-done
  132.8 0.4 project.1
  133.2 9.5 %all_to_all.30 = bf16[8,32,256]{2,1,0:T(8,128)(2,1)S(1)} all-to-all(bf16[8,32,256]{2,1,0:T(8,128)(2,1)S(1)} %project.1), channel_id=1, replica_groups=mesh['ctx'=64,'tp'=8] {'tp'}, dimensions={0} | all-to-all | bytes 262144 | tf_op jit(solution)/shard_map/all_to_all | solution.py:249
  142.7 0.6 reduce_sum.12
  (2 shorter events, 0.0 us)
Async XLA Ops:
  0.0 50.7 %copy-start.1 = (s32[128]{0:T(128)S(1)}, s32[128]{0:T(128)}, u32[]{:S(2)}) copy-start(s32[128]{0:T(128)} %len_ref.1) | copy-start | bytes 1540
  17.3 10.2 %copy-start.2 = (bf16[1,2048,128]{2,1,0:T(8,128)(2,1)S(1)}, bf16[1,2048,128]{2,1,0:T(8,128)(2,1)}, u32[]{:S(2)}) copy-start(bf16[1,2048,128]{2,1,0:T(8,128)(2,1)} %get-tuple-element.26) | copy-start | bytes 1572868 | tf_op jit(solution)/shard_map/cond
  17.3 10.4 %copy-start.4 = (bf16[1,2048,128]{2,1,0:T(8,128)(2,1)S(1)}, bf16[1,2048,128]{2,1,0:T(8,128)(2,1)}, u32[]{:S(2)}) copy-start(bf16[1,2048,128]{2,1,0:T(8,128)(2,1)} %get-tuple-element.28) | copy-start | bytes 1572868 | tf_op jit(solution)/shard_map/cond
  17.3 10.4 %copy-start.6 = (f32[1,2048]{1,0:T(1,128)S(1)}, f32[1,2048]{1,0:T(1,128)}, u32[]{:S(2)}) copy-start(f32[1,2048]{1,0:T(1,128)} %get-tuple-element.29) | copy-start | bytes 24580 | tf_op jit(solution)/shard_map/cond
  17.3 33.4 %all-to-all-start.1 = ((bf16[8,512,128]{2,1,0:T(8,128)(2,1)}), bf16[8,512,128]{2,1,0:T(8,128)(2,1)}, u32[]{:S(2)}, u32[]{:S(2)}) async-start(bf16[8,512,128]{2,1,0:T(8,128)(2,1)} %broadcast_in_dim.18), calls=%async_computation.1 | async-start | bytes 2097152 | tf_op jit(solution)/shard_map/cond/branch_0_fun/all_to_all | solution.py:194
  27.7 0.7 copy-start.8
  101.5 31.3 %copy-start = (bf16[2048,256]{1,0:T(8,128)(2,1)S(1)}, bf16[2048,256]{1,0:T(8,128)(2,1)}, u32[]{:S(2)}) copy-start(bf16[2048,256]{1,0:T(8,128)(2,1)} %w_ref.1) | copy-start | bytes 3145732

commit v3 on v2

--- a/solution.py
+++ b/solution.py
@@ -61,10 +61,10 @@
                     held = scores[slot][at : at + sub, :]
                     scores[slot][at : at + sub, :] = jnp.where(valid, held, NONE)
 
-    def weigh(group, slot):
+    def weigh(group, slot, half):
         kf = kf_ref[...]
         lane = iota((sub, width), 1)
-        for at in range(0, rows, sub):
+        for at in range(half * rows // 2, (half + 1) * rows // 2, sub):
             even, odd = limits(group, at // vectors)
             some = jnp.where(iota((sub, 1), 0) % 2 == 0, even, odd) > 0
             scaled = scores[slot][at : at + sub, :] * kf
@@ -74,8 +74,15 @@
             low = jnp.where(some, low, 0.0)
             marks[slot][at : at + sub, :] = jnp.where(lane == 0, high, low)
 
-    def gather(group, slot):
-        sums = jnp.dot(weights[slot][...], v_ref[...], preferred_element_type=F32)
+    def sums_of(slot, half):
+        own = weights[slot][half * rows // 2 : (half + 1) * rows // 2, :]
+        return jnp.dot(own, v_ref[...], preferred_element_type=F32)
+
+    def finish(group, slot):
+        weigh(group, slot, 0)
+        first = sums_of(slot, 0)
+        weigh(group, slot, 1)
+        sums = jnp.concatenate([first, sums_of(slot, 1)], axis=0)
         high, low = split_two(sums[:, width:])
         lane = iota((rows, width), 1)
         extra = jnp.where(lane < 2, marks[slot][...], jnp.where(lane == 2, high, low))
@@ -98,8 +105,7 @@
     def step(group, slot):
         mask(group - 1, 1 - slot)
         score(group, slot)
-        weigh(group - 1, 1 - slot)
-        gather(group - 1, 1 - slot)
+        finish(group - 1, 1 - slot)
 
     def pair(index, carry):
         step(2 * index, 0)
@@ -110,8 +116,7 @@
     step(1, 1)
     lax.fori_loop(1, groups // 2, pair, 0)
     mask(groups - 1, 1)
-    weigh(groups - 1, 1)
-    gather(groups - 1, 1)
+    finish(groups - 1, 1)
 
 
 def combine_kernel(in_ref, out_ref):
@@ -202,11 +207,15 @@
         value = jnp.concatenate([value, jnp.ones_like(value)], axis=1)
         return key_codes[0].T, key_scales * (LOG2E / math.sqrt(width)), value
 
+    def two_stages_first(own, memory):
+        query, memory = lax.optimization_barrier((two_stages(own), memory))
+        return query, prepare(*memory)
+
     memory = (key_codes, key_scales, value_codes, value_scales)
     query, (key_turned, key_factor, value) = lax.cond(
         lax.axis_index("tp") % 2 == 0,
         lambda own, memory: (direct(own), prepare(*memory)),
-        lambda own, memory: (two_stages(own), prepare(*memory)),
+        two_stages_first,
         own,
         memory,
     )

time: 144 us -> 141 us (0.979)
  blocking collectives: 87.8 us -> 120 us
  waiting for transfers between devices: 22.3 us -> 0 us
  starting transfers between devices: 10.2 us -> 0 us
  Pallas kernels: 19.6 us -> 17.9 us
    all_to_all x0 -> x1, blocking collectives: none -> 34.1 us  [two_stages(): lax.all_to_all(jnp.broadcast_to(line, (groups, sources * vectors, width))...]
    all_to_all x1 -> x0, waiting for transfers between devices: 22.3 us -> none  [two_stages(): lax.all_to_all(jnp.broadcast_to(line, (groups, sources * vectors, width))...]
    all_to_all x1 -> x0, starting transfers between devices: 10.2 us -> none  [two_stages(): lax.all_to_all(jnp.broadcast_to(line, (groups, sources * vectors, width))...]
    all_to_all x1, blocking collectives: 31.6 us -> 29.8 us  [local(): pieces = lax.all_to_all(partial, 'ctx', 0, 0, tiled=True)]
    pallas_call x1, Pallas kernels: 17.3 us -> 15.6 us  [local(): pl.pallas_call(attention_kernel, out_shape=jax.ShapeDtypeStruct((places,...]
  transfers between devices with their start and end apart: 1 -> 0, of which waited for: 1 -> 0; matrix products, arithmetic and copies ran while one was open for 0% -> 0% of each run, Pallas kernels for 0% -> 0%
where the time goes in v3:
time: 141 us; the launch traced here: 140 us
  blocking collectives  120 us (85%)
  Pallas kernels  17.9 us (13%)
    all_to_all x1, blocking collectives, two_stages(): lax.all_to_all(jnp.broadcast_to(line, (groups, sources * vectors, width))...  34.1 us
    all_to_all x1, blocking collectives, local(): attended = lax.all_to_all(attended, 'ctx', 0, 0, tiled=True)  31 us
    all_to_all x1, blocking collectives, local(): pieces = lax.all_to_all(partial, 'ctx', 0, 0, tiled=True)  29.8 us
    pallas_call x1, Pallas kernels, local(): pl.pallas_call(attention_kernel, out_shape=jax.ShapeDtypeStruct((places,...  15.6 us
    all_to_all x1, blocking collectives, two_stages(): lax.all_to_all(jnp.broadcast_to(own, (sources, vectors, width)), 'ctx', 0...  15.4 us
    all_to_all x1, blocking collectives, local(): terms = lax.all_to_all(terms, 'tp', 0, 0, tiled=True)  9.49 us

profile of v3, /device:TPU:1, one launch (start us, length us, event | category | flops | bytes accessed | tf_op | source)
XLA Modules:
  0.0 140.1 jit_solution(8828559037653722932)
XLA Ops:
  0.0 0.0 copy-start.1
  0.0 51.2 %conditional.1 = (bf16[64,64,128]{2,1,0:T(8,128)(2,1)}, f32[1,2048]{1,0:T(1,128)S(1)}, bf16[2048,256]{1,0:T(8,128)(2,1)S(1)}, bf16[128,2048]{1,0:T(8,128)(2,1)S(1)}) conditional(s32[]{:T(128)} %convert_element_type.23, (bf16[16,2,2,128]{3,0,2,1:T(8,128)(2,1)}, bf16[1,2048,128]{2,1,0:T(8,128)(2,1)}, f32[1,2048]{1,0:T(1,128)}, ...), branch_computations={%region_0.1_spmd, %region_1.2_spmd} | conditional | flops 788480 | bytes 12198066 | solution.py:215
  0.0 0.7 copy.12
  0.8 15.4 %all_to_all.27 = bf16[8,64,128]{2,1,0:T(8,128)(2,1)S(1)} all-to-all(bf16[8,64,128]{2,1,0:T(8,128)(2,1)S(1)} %broadcast_in_dim.13), channel_id=1, replica_groups={{0,8,16,24,32,40,48,56},{64,72,80,88,96,104,112,120},{128,136,144,152,1..., dimensions={0} | all-to-all | bytes 262144 | tf_op jit(solution)/shard_map/cond/branch_0_fun/all_to_all | solution.py:194
  16.2 0.1 broadcast_in_dim.18
  16.3 0.0 copy-start.8
  16.3 0.0 copy-start.2
  16.3 0.0 copy-start.4
  16.3 0.0 copy-start.6
  16.3 34.1 %all_to_all.28 = bf16[8,512,128]{2,1,0:T(8,128)(2,1)} all-to-all(bf16[8,512,128]{2,1,0:T(8,128)(2,1)S(1)} %broadcast_in_dim.18), channel_id=1, replica_groups={{0,64,128,192,256,320,384,448},{8,72,136,200,264,328,392,456},{16,80,14..., dimensions={0} | all-to-all | bytes 2097152 | tf_op jit(solution)/shard_map/cond/branch_0_fun/all_to_all | solution.py:199
  50.4 0.0 copy-done.8
  50.5 0.0 copy-done.2
  50.5 0.2 copy.10
  50.7 0.0 copy-done.4
  50.7 0.0 copy-done.6
  50.7 0.3 fusion
  51.1 0.1 concatenate.4
  51.2 0.0 copy-done.1
  51.2 15.6 %attention.1 = bf16[64,72,128]{2,1,0:T(8,128)(2,1)S(1)} custom-call(s32[128]{0:T(128)S(1)} %copy-done.1, bf16[64,64,128]{2,1,0:T(8,128)(2,1)} %get-tuple-element.44.q_ref, bf16[128,2048]{1,0:T(8,128)(2,1)S(1)} %get-tuple-element.48.kt_ref, f32[1,2048]{1,0:T(1,128)S(1)} %get-tuple-element.46.kf_ref, bf16[2048,256]{1,0:T(8,128)(2,1)S(1)} %get-tuple-element.47.v_ref), custom_call_target="tpu_custom_call" | custom-call | flops 8589934592 | bytes 8388608 | tf_op jit(solution)/shard_map/attention/pallas_call | solution.py:225
  66.8 29.8 %all_to_all.29.in_ref = bf16[64,72,128]{2,1,0:T(8,128)(2,1)S(1)} all-to-all(bf16[64,72,128]{2,1,0:T(8,128)(2,1)S(1)} %attention.1), channel_id=1, replica_groups=mesh['ctx'=64,'tp'=8] {'ctx'}, dimensions={0} | all-to-all | bytes 2359296 | tf_op jit(solution)/shard_map/all_to_all | solution.py:242
  96.7 1.8 %combine.1 = bf16[64,64,128]{2,1,0:T(8,128)(2,1)S(1)} custom-call(bf16[64,72,128]{2,1,0:T(8,128)(2,1)S(1)} %all_to_all.29.in_ref), custom_call_target="tpu_custom_call" | custom-call | tf_op jit(solution)/shard_map/combine/pallas_call | solution.py:244
  98.5 0.0 copy-start
  98.5 31.0 %all_to_all.30 = bf16[64,64,128]{2,1,0:T(8,128)(2,1)S(1)} all-to-all(bf16[64,64,128]{2,1,0:T(8,128)(2,1)S(1)} %combine.1), channel_id=1, replica_groups=mesh['ctx'=64,'tp'=8] {'ctx'}, dimensions={0} | all-to-all | bytes 2097152 | tf_op jit(solution)/shard_map/all_to_all | solution.py:250
  129.6 0.0 copy-done
  129.6 0.4 project.1
  130.0 9.5 %all_to_all.31 = bf16[8,32,256]{2,1,0:T(8,128)(2,1)S(1)} all-to-all(bf16[8,32,256]{2,1,0:T(8,128)(2,1)S(1)} %project.1), channel_id=1, replica_groups=mesh['ctx'=64,'tp'=8] {'tp'}, dimensions={0} | all-to-all | bytes 262144 | tf_op jit(solution)/shard_map/all_to_all | solution.py:258
  139.5 0.6 reduce_sum.12
  (2 shorter events, 0.0 us)
Async XLA Ops:
  0.0 51.2 %copy-start.1 = (s32[128]{0:T(128)S(1)}, s32[128]{0:T(128)}, u32[]{:S(2)}) copy-start(s32[128]{0:T(128)} %len_ref.1) | copy-start | bytes 1540
  16.3 34.2 %copy-start.8 = (f32[1,2048]{1,0:T(1,128)S(1)}, f32[1,2048]{1,0:T(1,128)}, u32[]{:S(2)}) copy-start(f32[1,2048]{1,0:T(1,128)} %get-tuple-element.32) | copy-start | bytes 24580 | tf_op jit(solution)/shard_map/cond
  16.3 34.2 %copy-start.2 = (bf16[1,2048,128]{2,1,0:T(8,128)(2,1)S(1)}, bf16[1,2048,128]{2,1,0:T(8,128)(2,1)}, u32[]{:S(2)}) copy-start(bf16[1,2048,128]{2,1,0:T(8,128)(2,1)} %get-tuple-element.31) | copy-start | bytes 1572868 | tf_op jit(solution)/shard_map/cond
  16.3 34.4 %copy-start.4 = (bf16[1,2048,128]{2,1,0:T(8,128)(2,1)S(1)}, bf16[1,2048,128]{2,1,0:T(8,128)(2,1)}, u32[]{:S(2)}) copy-start(bf16[1,2048,128]{2,1,0:T(8,128)(2,1)} %get-tuple-element.33) | copy-start | bytes 1572868 | tf_op jit(solution)/shard_map/cond
  16.3 34.4 %copy-start.6 = (f32[1,2048]{1,0:T(1,128)S(1)}, f32[1,2048]{1,0:T(1,128)}, u32[]{:S(2)}) copy-start(f32[1,2048]{1,0:T(1,128)} %get-tuple-element.34) | copy-start | bytes 24580 | tf_op jit(solution)/shard_map/cond
  98.5 31.1 %copy-start = (bf16[2048,256]{1,0:T(8,128)(2,1)S(1)}, bf16[2048,256]{1,0:T(8,128)(2,1)}, u32[]{:S(2)}) copy-start(bf16[2048,256]{1,0:T(8,128)(2,1)} %w_ref.1) | copy-start | bytes 3145732

commit v4 on v3

--- a/solution.py
+++ b/solution.py
@@ -26,7 +26,8 @@
 
 
 def attention_kernel(
-    len_ref, q_ref, kt_ref, kf_ref, v_ref, out_ref, s_even, s_odd, p_even, p_odd, m_even, m_odd
+    len_ref, q_ref, kt_ref, kf_ref, v_ref, out_ref,
+    s_even, s_odd, p_even, p_odd, m_even, m_odd, e_even, e_odd,
 ):
     vectors, width = q_ref.shape[1:]
     tokens = kt_ref.shape[1]
@@ -37,6 +38,7 @@
     sub = 16
     start = lax.axis_index("ctx") * tokens
     scores, weights, marks = (s_even, s_odd), (p_even, p_odd), (m_even, m_odd)
+    extras_of = (e_even, e_odd)
 
     def limits(group, source):
         row = (group * sources + source) * 2
@@ -92,9 +94,13 @@
             block = jnp.concatenate([sums[at : at + 8, :width] for at in places], axis=0)
             out_ref[group * parts + part, :vectors, :] = block.astype(BF16)
             extras += [extra[at : at + 8, :] for at in places]
-        extras = jnp.concatenate(extras, axis=0).astype(BF16)
+        extras_of[slot][...] = jnp.concatenate(extras, axis=0).astype(BF16)
+
+    def emit(group, slot):
         pick = (iota((EXTRA, width), 0) == iota((EXTRA, width), 1)).astype(BF16)
-        turned = lax.dot_general(pick, extras, (((1,), (1,)), ((), ())), preferred_element_type=F32)
+        turned = lax.dot_general(
+            pick, extras_of[slot][...], (((1,), (1,)), ((), ())), preferred_element_type=F32
+        )
         for part in range(parts):
             at = part // 2 * width
             row = turned[:, at : at + width]
@@ -102,10 +108,12 @@
                 row = pltpu.roll(row, vectors, 1)
             out_ref[group * parts + part, vectors:, :] = row.astype(BF16)
 
-    def step(group, slot):
+    def step(group, slot, late=True):
         mask(group - 1, 1 - slot)
         score(group, slot)
         finish(group - 1, 1 - slot)
+        if late:
+            emit(group - 2, slot)
 
     def pair(index, carry):
         step(2 * index, 0)
@@ -113,10 +121,12 @@
         return carry
 
     score(0, 0)
-    step(1, 1)
+    step(1, 1, late=False)
     lax.fori_loop(1, groups // 2, pair, 0)
     mask(groups - 1, 1)
+    emit(groups - 2, 0)
     finish(groups - 1, 1)
+    emit(groups - 1, 1)
 
 
 def combine_kernel(in_ref, out_ref):
@@ -129,12 +139,12 @@
     column = iota((places * EXTRA, places), 0)
     wanted = iota((places * EXTRA, places), 1) * EXTRA
 
-    def kind(index):
-        pick = (column == wanted + index).astype(BF16)
+    def both_halves(index):
+        pick = ((column == wanted + index) | (column == wanted + index + 1)).astype(BF16)
         return jnp.dot(turned, pick, preferred_element_type=F32)
 
-    top = kind(0) + kind(1)
-    total = kind(2) + kind(3)
+    top = both_halves(0)
+    total = both_halves(2)
     factor = jnp.exp2(top - jnp.max(top, axis=1, keepdims=True))
     denom = jnp.sum(factor * total, axis=1, keepdims=True)
     numer = jnp.zeros((vectors, width), F32)
@@ -229,7 +239,8 @@
         out_specs=vmem,
         scratch_shapes=[pltpu.VMEM((block, tokens), F32)] * 2
         + [pltpu.VMEM((block, tokens), BF16)] * 2
-        + [pltpu.VMEM((block, width), F32)] * 2,
+        + [pltpu.VMEM((block, width), F32)] * 2
+        + [pltpu.VMEM((block, width), BF16)] * 2,
         compiler_params=pltpu.CompilerParams(vmem_limit_bytes=48 * 1024 * 1024),
         cost_estimate=pl.CostEstimate(
             flops=8 * places * vectors * tokens * width,

time: 141 us -> 140 us (level)
  no operation moved by 1% of the time
where the time goes in v4:
time: 140 us; the launch traced here: 139 us
  blocking collectives  120 us (86%)
  Pallas kernels  17.3 us (12%)
    all_to_all x1, blocking collectives, two_stages(): lax.all_to_all(jnp.broadcast_to(line, (groups, sources * vectors, width))...  34.1 us
    all_to_all x1, blocking collectives, local(): attended = lax.all_to_all(attended, 'ctx', 0, 0, tiled=True)  31.1 us
    all_to_all x1, blocking collectives, local(): pieces = lax.all_to_all(partial, 'ctx', 0, 0, tiled=True)  29.7 us
    all_to_all x1, blocking collectives, two_stages(): lax.all_to_all(jnp.broadcast_to(own, (sources, vectors, width)), 'ctx', 0...  15.4 us
    pallas_call x1, Pallas kernels, local(): pl.pallas_call(attention_kernel, out_shape=jax.ShapeDtypeStruct((places,...  15 us
    all_to_all x1, blocking collectives, local(): terms = lax.all_to_all(terms, 'tp', 0, 0, tiled=True)  9.47 us

profile of v4, /device:TPU:1, one launch (start us, length us, event | category | flops | bytes accessed | tf_op | source)
XLA Modules:
  0.0 139.3 jit_solution(15761747913062015594)
XLA Ops:
  0.0 0.0 copy-start.1
  0.0 51.2 %conditional.1 = (bf16[64,64,128]{2,1,0:T(8,128)(2,1)}, f32[1,2048]{1,0:T(1,128)S(1)}, bf16[2048,256]{1,0:T(8,128)(2,1)S(1)}, bf16[128,2048]{1,0:T(8,128)(2,1)S(1)}) conditional(s32[]{:T(128)} %convert_element_type.23, (bf16[16,2,2,128]{3,0,2,1:T(8,128)(2,1)}, bf16[1,2048,128]{2,1,0:T(8,128)(2,1)}, f32[1,2048]{1,0:T(1,128)}, ...), branch_computations={%region_0.1_spmd, %region_1.2_spmd} | conditional | flops 788480 | bytes 12198066 | solution.py:225
  0.0 0.7 copy.12
  0.8 15.4 %all_to_all.27 = bf16[8,64,128]{2,1,0:T(8,128)(2,1)S(1)} all-to-all(bf16[8,64,128]{2,1,0:T(8,128)(2,1)S(1)} %broadcast_in_dim.13), channel_id=1, replica_groups={{0,8,16,24,32,40,48,56},{64,72,80,88,96,104,112,120},{128,136,144,152,1..., dimensions={0} | all-to-all | bytes 262144 | tf_op jit(solution)/shard_map/cond/branch_0_fun/all_to_all | solution.py:204
  16.2 0.1 broadcast_in_dim.18
  16.3 0.0 copy-start.8
  16.3 0.0 copy-start.2
  16.3 0.0 copy-start.4
  16.3 0.0 copy-start.6
  16.3 34.1 %all_to_all.28 = bf16[8,512,128]{2,1,0:T(8,128)(2,1)} all-to-all(bf16[8,512,128]{2,1,0:T(8,128)(2,1)S(1)} %broadcast_in_dim.18), channel_id=1, replica_groups={{0,64,128,192,256,320,384,448},{8,72,136,200,264,328,392,456},{16,80,14..., dimensions={0} | all-to-all | bytes 2097152 | tf_op jit(solution)/shard_map/cond/branch_0_fun/all_to_all | solution.py:209
  50.4 0.0 copy-done.8
  50.5 0.0 copy-done.2
  50.5 0.2 copy.10
  50.7 0.0 copy-done.4
  50.7 0.0 copy-done.6
  50.7 0.3 fusion
  51.1 0.1 concatenate.4
  51.2 0.0 copy-done.1
  51.2 15.0 %attention.1 = bf16[64,72,128]{2,1,0:T(8,128)(2,1)S(1)} custom-call(s32[128]{0:T(128)S(1)} %copy-done.1, bf16[64,64,128]{2,1,0:T(8,128)(2,1)} %get-tuple-element.44.q_ref, bf16[128,2048]{1,0:T(8,128)(2,1)S(1)} %get-tuple-element.48.kt_ref, f32[1,2048]{1,0:T(1,128)S(1)} %get-tuple-element.46.kf_ref, bf16[2048,256]{1,0:T(8,128)(2,1)S(1)} %get-tuple-element.47.v_ref), custom_call_target="tpu_custom_call" | custom-call | flops 8589934592 | bytes 8388608 | tf_op jit(solution)/shard_map/attention/pallas_call | solution.py:235
  66.2 29.7 %all_to_all.29.in_ref = bf16[64,72,128]{2,1,0:T(8,128)(2,1)S(1)} all-to-all(bf16[64,72,128]{2,1,0:T(8,128)(2,1)S(1)} %attention.1), channel_id=1, replica_groups=mesh['ctx'=64,'tp'=8] {'ctx'}, dimensions={0} | all-to-all | bytes 2359296 | tf_op jit(solution)/shard_map/all_to_all | solution.py:253
  95.9 1.8 %combine.1 = bf16[64,64,128]{2,1,0:T(8,128)(2,1)S(1)} custom-call(bf16[64,72,128]{2,1,0:T(8,128)(2,1)S(1)} %all_to_all.29.in_ref), custom_call_target="tpu_custom_call" | custom-call | tf_op jit(solution)/shard_map/combine/pallas_call | solution.py:255
  97.7 0.0 copy-start
  97.7 31.1 %all_to_all.30 = bf16[64,64,128]{2,1,0:T(8,128)(2,1)S(1)} all-to-all(bf16[64,64,128]{2,1,0:T(8,128)(2,1)S(1)} %combine.1), channel_id=1, replica_groups=mesh['ctx'=64,'tp'=8] {'ctx'}, dimensions={0} | all-to-all | bytes 2097152 | tf_op jit(solution)/shard_map/all_to_all | solution.py:261
  128.8 0.0 copy-done
  128.8 0.4 project.1
  129.2 9.5 %all_to_all.31 = bf16[8,32,256]{2,1,0:T(8,128)(2,1)S(1)} all-to-all(bf16[8,32,256]{2,1,0:T(8,128)(2,1)S(1)} %project.1), channel_id=1, replica_groups=mesh['ctx'=64,'tp'=8] {'tp'}, dimensions={0} | all-to-all | bytes 262144 | tf_op jit(solution)/shard_map/all_to_all | solution.py:269
  138.7 0.6 reduce_sum.12
  (2 shorter events, 0.0 us)
Async XLA Ops:
  0.0 51.2 %copy-start.1 = (s32[128]{0:T(128)S(1)}, s32[128]{0:T(128)}, u32[]{:S(2)}) copy-start(s32[128]{0:T(128)} %len_ref.1) | copy-start | bytes 1540
  16.3 34.2 %copy-start.8 = (f32[1,2048]{1,0:T(1,128)S(1)}, f32[1,2048]{1,0:T(1,128)}, u32[]{:S(2)}) copy-start(f32[1,2048]{1,0:T(1,128)} %get-tuple-element.32) | copy-start | bytes 24580 | tf_op jit(solution)/shard_map/cond
  16.3 34.2 %copy-start.2 = (bf16[1,2048,128]{2,1,0:T(8,128)(2,1)S(1)}, bf16[1,2048,128]{2,1,0:T(8,128)(2,1)}, u32[]{:S(2)}) copy-start(bf16[1,2048,128]{2,1,0:T(8,128)(2,1)} %get-tuple-element.31) | copy-start | bytes 1572868 | tf_op jit(solution)/shard_map/cond
  16.3 34.4 %copy-start.4 = (bf16[1,2048,128]{2,1,0:T(8,128)(2,1)S(1)}, bf16[1,2048,128]{2,1,0:T(8,128)(2,1)}, u32[]{:S(2)}) copy-start(bf16[1,2048,128]{2,1,0:T(8,128)(2,1)} %get-tuple-element.33) | copy-start | bytes 1572868 | tf_op jit(solution)/shard_map/cond
  16.3 34.4 %copy-start.6 = (f32[1,2048]{1,0:T(1,128)S(1)}, f32[1,2048]{1,0:T(1,128)}, u32[]{:S(2)}) copy-start(f32[1,2048]{1,0:T(1,128)} %get-tuple-element.34) | copy-start | bytes 24580 | tf_op jit(solution)/shard_map/cond
  97.7 31.1 %copy-start = (bf16[2048,256]{1,0:T(8,128)(2,1)S(1)}, bf16[2048,256]{1,0:T(8,128)(2,1)}, u32[]{:S(2)}) copy-start(bf16[2048,256]{1,0:T(8,128)(2,1)} %w_ref.1) | copy-start | bytes 3145732

commit v5 on v4

--- a/solution.py
+++ b/solution.py
@@ -223,7 +223,7 @@
 
     memory = (key_codes, key_scales, value_codes, value_scales)
     query, (key_turned, key_factor, value) = lax.cond(
-        lax.axis_index("tp") % 2 == 0,
+        lax.axis_index("tp") % 2 == 1,
         lambda own, memory: (direct(own), prepare(*memory)),
         two_stages_first,
         own,

time: 140 us -> 134 us (0.957)
  blocking collectives: 120 us -> 76.9 us
  waiting for transfers between devices: 0 us -> 17.8 us
  starting transfers between devices: 0 us -> 17.5 us
    all_to_all x2 -> x0, blocking collectives: 49.5 us -> none  [the longest x1 34.1 us: two_stages(): lax.all_to_all(jnp.broadcast_to(line, (groups, sources * vectors, width))...]
    all_to_all x0 -> x1, waiting for transfers between devices: none -> 17.8 us  [direct(): lax.all_to_all(jnp.broadcast_to(own, (places, vectors, width)), 'ctx', 0,...]
    all_to_all x0 -> x1, starting transfers between devices: none -> 17.5 us  [direct(): lax.all_to_all(jnp.broadcast_to(own, (places, vectors, width)), 'ctx', 0,...]
    all_to_all x1, blocking collectives: 9.47 us -> 24.1 us  [local(): terms = lax.all_to_all(terms, 'tp', 0, 0, tiled=True)]
    all_to_all x1, blocking collectives: 31.1 us -> 25.1 us  [local(): attended = lax.all_to_all(attended, 'ctx', 0, 0, tiled=True)]
    all_to_all x1, blocking collectives: 29.7 us -> 27.7 us  [local(): pieces = lax.all_to_all(partial, 'ctx', 0, 0, tiled=True)]
  transfers between devices with their start and end apart: 0 -> 1, of which waited for: 0 -> 1; matrix products, arithmetic and copies ran while one was open for 0% -> 1% of each run, Pallas kernels for 0% -> 0%
where the time goes in v5:
time: 134 us; the launch traced here: 133 us
  blocking collectives  76.9 us (57%)
  waiting for transfers between devices  17.8 us (13%)
  starting transfers between devices  17.5 us (13%)
  Pallas kernels  17.3 us (13%)
  local copies, waits for them, and re-layouts  2.56 us (2%)
    all_to_all x1, blocking collectives, local(): pieces = lax.all_to_all(partial, 'ctx', 0, 0, tiled=True)  27.7 us
    all_to_all x1, blocking collectives, local(): attended = lax.all_to_all(attended, 'ctx', 0, 0, tiled=True)  25.1 us
    all_to_all x1, blocking collectives, local(): terms = lax.all_to_all(terms, 'tp', 0, 0, tiled=True)  24.1 us
    all_to_all x1, waiting for transfers between devices, direct(): lax.all_to_all(jnp.broadcast_to(own, (places, vectors, width)), 'ctx', 0,...  17.8 us
    all_to_all x1, starting transfers between devices, direct(): lax.all_to_all(jnp.broadcast_to(own, (places, vectors, width)), 'ctx', 0,...  17.5 us
    pallas_call x1, Pallas kernels, local(): pl.pallas_call(attention_kernel, out_shape=jax.ShapeDtypeStruct((places,...  15 us
  transfers between devices with their start and end apart: 1, of which 1 were waited for; matrix products, arithmetic and copies ran while one was open for 1% of the time, Pallas kernels for 0%

profile of v5, /device:TPU:1, one launch (start us, length us, event | category | flops | bytes accessed | tf_op | source)
XLA Modules:
  0.0 133.1 jit_solution(6118641198721942005)
XLA Ops:
  0.0 0.0 copy-start.1
  0.0 38.3 %conditional.1 = (bf16[64,64,128]{2,1,0:T(8,128)(2,1)}, f32[1,2048]{1,0:T(1,128)S(1)}, bf16[2048,256]{1,0:T(8,128)(2,1)S(1)}, bf16[128,2048]{1,0:T(8,128)(2,1)S(1)}) conditional(s32[]{:T(128)} %convert_element_type.23, (bf16[16,2,2,128]{3,0,2,1:T(8,128)(2,1)}, bf16[1,2048,128]{2,1,0:T(8,128)(2,1)}, f32[1,2048]{1,0:T(1,128)}, ...), branch_computations={%region_0.1_spmd, %region_1.2_spmd} | conditional | flops 788480 | bytes 12198066 | solution.py:225
  0.0 0.7 copy.13
  0.7 1.2 broadcast_in_dim.20
  2.0 0.0 copy-start.3
  2.0 0.0 copy-start.5
  2.0 0.0 copy-start.7
  2.0 17.5 %all-to-all-start.2 = ((bf16[64,64,128]{2,1,0:T(8,128)(2,1)}), bf16[64,64,128]{2,1,0:T(8,128)(2,1)}, u32[]{:S(2)}, u32[]{:S(2)}) async-start(bf16[64,64,128]{2,1,0:T(8,128)(2,1)} %broadcast_in_dim.20), calls=%async_computation.2 | async-start | bytes 2097152 | tf_op jit(solution)/shard_map/cond/branch_1_fun/all_to_all | solution.py:197
  19.5 0.0 copy-done.3
  19.5 0.2 copy.11
  19.8 0.0 copy-done.5
  19.8 0.0 copy-done.7
  19.8 0.0 copy-start.9
  19.8 0.3 fusion.1
  20.1 0.1 concatenate.5
  20.2 0.2 copy-done.9
  20.5 17.8 %all-to-all-done.2 = bf16[64,64,128]{2,1,0:T(8,128)(2,1)} async-done(((bf16[64,64,128]{2,1,0:T(8,128)(2,1)}), bf16[64,64,128]{2,1,0:T(8,128)(2,1)}, u32[]{:S(2)}, u32[]{:S(2)}) %all-to-all-start.2) | async-done | bytes 1048608 | tf_op jit(solution)/shard_map/cond/branch_1_fun/all_to_all | solution.py:197
  38.3 0.0 copy-done.1
  38.3 15.0 %attention.1 = bf16[64,72,128]{2,1,0:T(8,128)(2,1)S(1)} custom-call(s32[128]{0:T(128)S(1)} %copy-done.1, bf16[64,64,128]{2,1,0:T(8,128)(2,1)} %get-tuple-element.44.q_ref, bf16[128,2048]{1,0:T(8,128)(2,1)S(1)} %get-tuple-element.48.kt_ref, f32[1,2048]{1,0:T(1,128)S(1)} %get-tuple-element.46.kf_ref, bf16[2048,256]{1,0:T(8,128)(2,1)S(1)} %get-tuple-element.47.v_ref), custom_call_target="tpu_custom_call" | custom-call | flops 8589934592 | bytes 8388608 | tf_op jit(solution)/shard_map/attention/pallas_call | solution.py:235
  53.3 27.7 %all_to_all.29.in_ref = bf16[64,72,128]{2,1,0:T(8,128)(2,1)S(1)} all-to-all(bf16[64,72,128]{2,1,0:T(8,128)(2,1)S(1)} %attention.1), channel_id=1, replica_groups=mesh['ctx'=64,'tp'=8] {'ctx'}, dimensions={0} | all-to-all | bytes 2359296 | tf_op jit(solution)/shard_map/all_to_all | solution.py:253
  81.0 1.8 %combine.1 = bf16[64,64,128]{2,1,0:T(8,128)(2,1)S(1)} custom-call(bf16[64,72,128]{2,1,0:T(8,128)(2,1)S(1)} %all_to_all.29.in_ref), custom_call_target="tpu_custom_call" | custom-call | tf_op jit(solution)/shard_map/combine/pallas_call | solution.py:255
  82.8 0.0 copy-start
  82.8 25.1 %all_to_all.30 = bf16[64,64,128]{2,1,0:T(8,128)(2,1)S(1)} all-to-all(bf16[64,64,128]{2,1,0:T(8,128)(2,1)S(1)} %combine.1), channel_id=1, replica_groups=mesh['ctx'=64,'tp'=8] {'ctx'}, dimensions={0} | all-to-all | bytes 2097152 | tf_op jit(solution)/shard_map/all_to_all | solution.py:261
  107.9 0.0 copy-done
  107.9 0.4 project.1
  108.4 24.1 %all_to_all.31 = bf16[8,32,256]{2,1,0:T(8,128)(2,1)S(1)} all-to-all(bf16[8,32,256]{2,1,0:T(8,128)(2,1)S(1)} %project.1), channel_id=1, replica_groups=mesh['ctx'=64,'tp'=8] {'tp'}, dimensions={0} | all-to-all | bytes 262144 | tf_op jit(solution)/shard_map/all_to_all | solution.py:269
  132.5 0.6 reduce_sum.12
  (1 shorter events, 0.0 us)
Async XLA Ops:
  0.0 38.3 %copy-start.1 = (s32[128]{0:T(128)S(1)}, s32[128]{0:T(128)}, u32[]{:S(2)}) copy-start(s32[128]{0:T(128)} %len_ref.1) | copy-start | bytes 1540
  2.0 17.5 %copy-start.3 = (bf16[1,2048,128]{2,1,0:T(8,128)(2,1)S(1)}, bf16[1,2048,128]{2,1,0:T(8,128)(2,1)}, u32[]{:S(2)}) copy-start(bf16[1,2048,128]{2,1,0:T(8,128)(2,1)} %get-tuple-element.36) | copy-start | bytes 1572868 | tf_op jit(solution)/shard_map/cond
  2.0 17.8 %copy-start.5 = (bf16[1,2048,128]{2,1,0:T(8,128)(2,1)S(1)}, bf16[1,2048,128]{2,1,0:T(8,128)(2,1)}, u32[]{:S(2)}) copy-start(bf16[1,2048,128]{2,1,0:T(8,128)(2,1)} %get-tuple-element.38) | copy-start | bytes 1572868 | tf_op jit(solution)/shard_map/cond
  2.0 17.8 %copy-start.7 = (f32[1,2048]{1,0:T(1,128)S(1)}, f32[1,2048]{1,0:T(1,128)}, u32[]{:S(2)}) copy-start(f32[1,2048]{1,0:T(1,128)} %get-tuple-element.39) | copy-start | bytes 24580 | tf_op jit(solution)/shard_map/cond
  2.0 36.3 %all-to-all-start.2 = ((bf16[64,64,128]{2,1,0:T(8,128)(2,1)}), bf16[64,64,128]{2,1,0:T(8,128)(2,1)}, u32[]{:S(2)}, u32[]{:S(2)}) async-start(bf16[64,64,128]{2,1,0:T(8,128)(2,1)} %broadcast_in_dim.20), calls=%async_computation.2 | async-start | bytes 2097152 | tf_op jit(solution)/shard_map/cond/branch_1_fun/all_to_all | solution.py:197
  19.8 0.7 copy-start.9
  82.8 25.1 %copy-start = (bf16[2048,256]{1,0:T(8,128)(2,1)S(1)}, bf16[2048,256]{1,0:T(8,128)(2,1)}, u32[]{:S(2)}) copy-start(bf16[2048,256]{1,0:T(8,128)(2,1)} %w_ref.1) | copy-start | bytes 3145732

commit v6 on v5

--- a/solution.py
+++ b/solution.py
@@ -129,6 +129,18 @@
     emit(groups - 1, 1)
 
 
+def spread_kernel(in_ref, out_ref):
+    steps, rows, heads, width = in_ref.shape
+    vectors = steps * rows * heads
+    new = iota((vectors, vectors), 0)
+    old = iota((vectors, vectors), 1)
+    pick = (old == new % (steps * rows) * heads + new // (steps * rows)).astype(BF16)
+    own = in_ref[...].reshape(vectors, width)
+    own = jnp.dot(pick, own, preferred_element_type=F32).astype(BF16)
+    for at in range(out_ref.shape[0]):
+        out_ref[at] = own
+
+
 def combine_kernel(in_ref, out_ref):
     places, total_rows, width = in_ref.shape
     vectors = total_rows - EXTRA
@@ -155,8 +167,13 @@
     common = common ^ (common >> 4)
     common = common ^ (common >> 2)
     common = common ^ (common >> 1)
-    signs = (1 - 2 * (common & 1)).astype(F32)
-    attended = jnp.dot(rotated, signs, precision=lax.Precision.HIGHEST, preferred_element_type=F32)
+    signs = (1 - 2 * (common & 1)).astype(BF16)
+    attended = jnp.zeros((vectors, width), F32)
+    rest = rotated
+    for _ in range(3):
+        piece = rest.astype(BF16)
+        rest = rest - piece.astype(F32)
+        attended = attended + jnp.dot(piece, signs, preferred_element_type=F32)
     attended = (attended * (1.0 / math.sqrt(width))).astype(BF16)
     new = iota((vectors, vectors), 0)
     old = iota((vectors, vectors), 1)
@@ -202,7 +219,11 @@
         lines = [[at * sources + i for i in range(sources)] for at in range(groups)]
         across = [[i * sources + at for i in range(groups)] for at in range(sources)]
         line = lax.all_to_all(
-            jnp.broadcast_to(own, (sources, vectors, width)),
+            pl.pallas_call(
+                spread_kernel,
+                out_shape=jax.ShapeDtypeStruct((sources, vectors, width), BF16),
+                name="spread",
+            )(queries),
             "ctx", 0, 0, axis_index_groups=lines, tiled=True,
         )
         line = line.reshape(1, sources * vectors, width)

time: 134 us -> 134 us (level)
  no operation moved by 1% of the time
where the time goes in v6:
time: 134 us; the launch traced here: 133 us
  blocking collectives  76.9 us (57%)
  waiting for transfers between devices  17.7 us (13%)
  starting transfers between devices  17.5 us (13%)
  Pallas kernels  17.2 us (13%)
  local copies, waits for them, and re-layouts  2.55 us (2%)
    all_to_all x1, blocking collectives, local(): pieces = lax.all_to_all(partial, 'ctx', 0, 0, tiled=True)  27.7 us
    all_to_all x1, blocking collectives, local(): attended = lax.all_to_all(attended, 'ctx', 0, 0, tiled=True)  25.2 us
    all_to_all x1, blocking collectives, local(): terms = lax.all_to_all(terms, 'tp', 0, 0, tiled=True)  24 us
    all_to_all x1, waiting for transfers between devices, direct(): lax.all_to_all(jnp.broadcast_to(own, (places, vectors, width)), 'ctx', 0,...  17.7 us
    all_to_all x1, starting transfers between devices, direct(): lax.all_to_all(jnp.broadcast_to(own, (places, vectors, width)), 'ctx', 0,...  17.5 us
    pallas_call x1, Pallas kernels, local(): pl.pallas_call(attention_kernel, out_shape=jax.ShapeDtypeStruct((places,...  15 us
  transfers between devices with their start and end apart: 1, of which 1 were waited for; matrix products, arithmetic and copies ran while one was open for 1% of the time, Pallas kernels for 0%

profile of v6, /device:TPU:1, one launch (start us, length us, event | category | flops | bytes accessed | tf_op | source)
XLA Modules:
  0.0 132.9 jit_solution(16971424242300461868)
XLA Ops:
  0.0 0.7 copy.13
  0.7 0.0 copy-start.1
  0.7 37.5 %conditional.1 = (bf16[64,64,128]{2,1,0:T(8,128)(2,1)}, f32[1,2048]{1,0:T(1,128)S(1)}, bf16[2048,256]{1,0:T(8,128)(2,1)S(1)}, bf16[128,2048]{1,0:T(8,128)(2,1)S(1)}) conditional(s32[]{:T(128)} %convert_element_type.23, (bf16[2,2,16,128]{3,2,1,0:T(8,128)(2,1)}, bf16[1,2048,128]{2,1,0:T(8,128)(2,1)}, f32[1,2048]{1,0:T(1,128)}, ...), branch_computations={%region_0.1_spmd, %region_1.2_spmd} | conditional | flops 788480 | bytes 12165298 | solution.py:246
  0.8 1.2 broadcast_in_dim.13
  2.0 0.0 copy-start.3
  2.0 0.0 copy-start.5
  2.0 0.0 copy-start.7
  2.0 17.5 %all-to-all-start.2 = ((bf16[64,64,128]{2,1,0:T(8,128)(2,1)}), bf16[64,64,128]{2,1,0:T(8,128)(2,1)}, u32[]{:S(2)}, u32[]{:S(2)}) async-start(bf16[64,64,128]{2,1,0:T(8,128)(2,1)} %broadcast_in_dim.13), calls=%async_computation.2 | async-start | bytes 2097152 | tf_op jit(solution)/shard_map/cond/branch_1_fun/all_to_all | solution.py:214
  19.5 0.0 copy-done.3
  19.6 0.2 copy.11
  19.8 0.0 copy-done.5
  19.8 0.0 copy-done.7
  19.8 0.0 copy-start.9
  19.8 0.3 fusion.1
  20.2 0.1 concatenate.5
  20.3 0.2 copy-done.9
  20.5 17.7 %all-to-all-done.2 = bf16[64,64,128]{2,1,0:T(8,128)(2,1)} async-done(((bf16[64,64,128]{2,1,0:T(8,128)(2,1)}), bf16[64,64,128]{2,1,0:T(8,128)(2,1)}, u32[]{:S(2)}, u32[]{:S(2)}) %all-to-all-start.2) | async-done | bytes 1048608 | tf_op jit(solution)/shard_map/cond/branch_1_fun/all_to_all | solution.py:214
  38.2 0.0 copy-done.1
  38.2 15.0 %attention.1 = bf16[64,72,128]{2,1,0:T(8,128)(2,1)S(1)} custom-call(s32[128]{0:T(128)S(1)} %copy-done.1, bf16[64,64,128]{2,1,0:T(8,128)(2,1)} %get-tuple-element.45.q_ref, bf16[128,2048]{1,0:T(8,128)(2,1)S(1)} %get-tuple-element.49.kt_ref, f32[1,2048]{1,0:T(1,128)S(1)} %get-tuple-element.47.kf_ref, bf16[2048,256]{1,0:T(8,128)(2,1)S(1)} %get-tuple-element.48.v_ref), custom_call_target="tpu_custom_call" | custom-call | flops 8589934592 | bytes 8388608 | tf_op jit(solution)/shard_map/attention/pallas_call | solution.py:256
  53.2 27.7 %all_to_all.29.in_ref = bf16[64,72,128]{2,1,0:T(8,128)(2,1)S(1)} all-to-all(bf16[64,72,128]{2,1,0:T(8,128)(2,1)S(1)} %attention.1), channel_id=1, replica_groups=mesh['ctx'=64,'tp'=8] {'ctx'}, dimensions={0} | all-to-all | bytes 2359296 | tf_op jit(solution)/shard_map/all_to_all | solution.py:274
  81.0 1.7 %combine.1 = bf16[64,64,128]{2,1,0:T(8,128)(2,1)S(1)} custom-call(bf16[64,72,128]{2,1,0:T(8,128)(2,1)S(1)} %all_to_all.29.in_ref), custom_call_target="tpu_custom_call" | custom-call | tf_op jit(solution)/shard_map/combine/pallas_call | solution.py:276
  82.7 0.0 copy-start
  82.7 25.2 %all_to_all.30 = bf16[64,64,128]{2,1,0:T(8,128)(2,1)S(1)} all-to-all(bf16[64,64,128]{2,1,0:T(8,128)(2,1)S(1)} %combine.1), channel_id=1, replica_groups=mesh['ctx'=64,'tp'=8] {'ctx'}, dimensions={0} | all-to-all | bytes 2097152 | tf_op jit(solution)/shard_map/all_to_all | solution.py:282
  107.9 0.0 copy-done
  107.9 0.4 project.1
  108.3 24.0 %all_to_all.31 = bf16[8,32,256]{2,1,0:T(8,128)(2,1)S(1)} all-to-all(bf16[8,32,256]{2,1,0:T(8,128)(2,1)S(1)} %project.1), channel_id=1, replica_groups=mesh['ctx'=64,'tp'=8] {'tp'}, dimensions={0} | all-to-all | bytes 262144 | tf_op jit(solution)/shard_map/all_to_all | solution.py:290
  132.3 0.6 reduce_sum.12
  (1 shorter events, 0.0 us)
Async XLA Ops:
  0.7 37.5 %copy-start.1 = (s32[128]{0:T(128)S(1)}, s32[128]{0:T(128)}, u32[]{:S(2)}) copy-start(s32[128]{0:T(128)} %len_ref.1) | copy-start | bytes 1540
  2.0 17.5 %copy-start.3 = (bf16[1,2048,128]{2,1,0:T(8,128)(2,1)S(1)}, bf16[1,2048,128]{2,1,0:T(8,128)(2,1)}, u32[]{:S(2)}) copy-start(bf16[1,2048,128]{2,1,0:T(8,128)(2,1)} %get-tuple-element.37) | copy-start | bytes 1572868 | tf_op jit(solution)/shard_map/cond
  2.0 17.8 %copy-start.5 = (bf16[1,2048,128]{2,1,0:T(8,128)(2,1)S(1)}, bf16[1,2048,128]{2,1,0:T(8,128)(2,1)}, u32[]{:S(2)}) copy-start(bf16[1,2048,128]{2,1,0:T(8,128)(2,1)} %get-tuple-element.39) | copy-start | bytes 1572868 | tf_op jit(solution)/shard_map/cond
  2.0 17.8 %copy-start.7 = (f32[1,2048]{1,0:T(1,128)S(1)}, f32[1,2048]{1,0:T(1,128)}, u32[]{:S(2)}) copy-start(f32[1,2048]{1,0:T(1,128)} %get-tuple-element.40) | copy-start | bytes 24580 | tf_op jit(solution)/shard_map/cond
  2.0 36.2 %all-to-all-start.2 = ((bf16[64,64,128]{2,1,0:T(8,128)(2,1)}), bf16[64,64,128]{2,1,0:T(8,128)(2,1)}, u32[]{:S(2)}, u32[]{:S(2)}) async-start(bf16[64,64,128]{2,1,0:T(8,128)(2,1)} %broadcast_in_dim.13), calls=%async_computation.2 | async-start | bytes 2097152 | tf_op jit(solution)/shard_map/cond/branch_1_fun/all_to_all | solution.py:214
  19.8 0.7 copy-start.9
  82.7 25.2 %copy-start = (bf16[2048,256]{1,0:T(8,128)(2,1)S(1)}, bf16[2048,256]{1,0:T(8,128)(2,1)}, u32[]{:S(2)}) copy-start(bf16[2048,256]{1,0:T(8,128)(2,1)} %w_ref.1) | copy-start | bytes 3145732

commit v7 on v6

--- a/solution.py
+++ b/solution.py
@@ -35,7 +35,7 @@
     sources = rows // vectors
     groups = q_ref.shape[0] // sources
     parts = vectors // 8
-    sub = 16
+    sub = 32
     start = lax.axis_index("ctx") * tokens
     scores, weights, marks = (s_even, s_odd), (p_even, p_odd), (m_even, m_odd)
     extras_of = (e_even, e_odd)

time: 134 us -> 133 us (level)
  no operation moved by 1% of the time
where the time goes in v7:
time: 133 us
  blocking collectives  76.9 us (58%)
  waiting for transfers between devices  17.7 us (13%)
  starting transfers between devices  17.5 us (13%)
  Pallas kernels  17.2 us (13%)
  local copies, waits for them, and re-layouts  2.55 us (2%)
    all_to_all x1, blocking collectives, local(): pieces = lax.all_to_all(partial, 'ctx', 0, 0, tiled=True)  27.8 us
    all_to_all x1, blocking collectives, local(): attended = lax.all_to_all(attended, 'ctx', 0, 0, tiled=True)  25.2 us
    all_to_all x1, blocking collectives, local(): terms = lax.all_to_all(terms, 'tp', 0, 0, tiled=True)  23.8 us
    all_to_all x1, waiting for transfers between devices, direct(): lax.all_to_all(jnp.broadcast_to(own, (places, vectors, width)), 'ctx', 0,...  17.7 us
    all_to_all x1, starting transfers between devices, direct(): lax.all_to_all(jnp.broadcast_to(own, (places, vectors, width)), 'ctx', 0,...  17.5 us
    pallas_call x1, Pallas kernels, local(): pl.pallas_call(attention_kernel, out_shape=jax.ShapeDtypeStruct((places,...  15.1 us
  transfers between devices with their start and end apart: 1, of which 1 were waited for; matrix products, arithmetic and copies ran while one was open for 1% of the time, Pallas kernels for 0%

profile of v7, /device:TPU:1, one launch (start us, length us, event | category | flops | bytes accessed | tf_op | source)
XLA Modules:
  0.0 133.0 jit_solution(18295419125792022557)
XLA Ops:
  0.0 0.7 copy.13
  0.7 0.0 copy-start.1
  0.7 37.5 %conditional.1 = (bf16[64,64,128]{2,1,0:T(8,128)(2,1)}, f32[1,2048]{1,0:T(1,128)S(1)}, bf16[2048,256]{1,0:T(8,128)(2,1)S(1)}, bf16[128,2048]{1,0:T(8,128)(2,1)S(1)}) conditional(s32[]{:T(128)} %convert_element_type.23, (bf16[2,2,16,128]{3,2,1,0:T(8,128)(2,1)}, bf16[1,2048,128]{2,1,0:T(8,128)(2,1)}, f32[1,2048]{1,0:T(1,128)}, ...), branch_computations={%region_0.1_spmd, %region_1.2_spmd} | conditional | flops 788480 | bytes 12165298 | solution.py:246
  0.8 1.2 broadcast_in_dim.13
  2.0 0.0 copy-start.3
  2.0 0.0 copy-start.5
  2.0 0.0 copy-start.7
  2.0 17.5 %all-to-all-start.2 = ((bf16[64,64,128]{2,1,0:T(8,128)(2,1)}), bf16[64,64,128]{2,1,0:T(8,128)(2,1)}, u32[]{:S(2)}, u32[]{:S(2)}) async-start(bf16[64,64,128]{2,1,0:T(8,128)(2,1)} %broadcast_in_dim.13), calls=%async_computation.2 | async-start | bytes 2097152 | tf_op jit(solution)/shard_map/cond/branch_1_fun/all_to_all | solution.py:214
  19.5 0.0 copy-done.3
  19.6 0.2 copy.11
  19.8 0.0 copy-done.5
  19.8 0.0 copy-done.7
  19.8 0.0 copy-start.9
  19.8 0.3 fusion.1
  20.2 0.1 concatenate.5
  20.3 0.2 copy-done.9
  20.5 17.7 %all-to-all-done.2 = bf16[64,64,128]{2,1,0:T(8,128)(2,1)} async-done(((bf16[64,64,128]{2,1,0:T(8,128)(2,1)}), bf16[64,64,128]{2,1,0:T(8,128)(2,1)}, u32[]{:S(2)}, u32[]{:S(2)}) %all-to-all-start.2) | async-done | bytes 1048608 | tf_op jit(solution)/shard_map/cond/branch_1_fun/all_to_all | solution.py:214
  38.2 0.0 copy-done.1
  38.2 15.1 %attention.1 = bf16[64,72,128]{2,1,0:T(8,128)(2,1)S(1)} custom-call(s32[128]{0:T(128)S(1)} %copy-done.1, bf16[64,64,128]{2,1,0:T(8,128)(2,1)} %get-tuple-element.45.q_ref, bf16[128,2048]{1,0:T(8,128)(2,1)S(1)} %get-tuple-element.49.kt_ref, f32[1,2048]{1,0:T(1,128)S(1)} %get-tuple-element.47.kf_ref, bf16[2048,256]{1,0:T(8,128)(2,1)S(1)} %get-tuple-element.48.v_ref), custom_call_target="tpu_custom_call" | custom-call | flops 8589934592 | bytes 8388608 | tf_op jit(solution)/shard_map/attention/pallas_call | solution.py:256
  53.3 27.8 %all_to_all.29.in_ref = bf16[64,72,128]{2,1,0:T(8,128)(2,1)S(1)} all-to-all(bf16[64,72,128]{2,1,0:T(8,128)(2,1)S(1)} %attention.1), channel_id=1, replica_groups=mesh['ctx'=64,'tp'=8] {'ctx'}, dimensions={0} | all-to-all | bytes 2359296 | tf_op jit(solution)/shard_map/all_to_all | solution.py:274
  81.1 1.7 %combine.1 = bf16[64,64,128]{2,1,0:T(8,128)(2,1)S(1)} custom-call(bf16[64,72,128]{2,1,0:T(8,128)(2,1)S(1)} %all_to_all.29.in_ref), custom_call_target="tpu_custom_call" | custom-call | tf_op jit(solution)/shard_map/combine/pallas_call | solution.py:276
  82.8 0.0 copy-start
  82.8 25.2 %all_to_all.30 = bf16[64,64,128]{2,1,0:T(8,128)(2,1)S(1)} all-to-all(bf16[64,64,128]{2,1,0:T(8,128)(2,1)S(1)} %combine.1), channel_id=1, replica_groups=mesh['ctx'=64,'tp'=8] {'ctx'}, dimensions={0} | all-to-all | bytes 2097152 | tf_op jit(solution)/shard_map/all_to_all | solution.py:282
  108.1 0.0 copy-done
  108.1 0.4 project.1
  108.5 23.8 %all_to_all.31 = bf16[8,32,256]{2,1,0:T(8,128)(2,1)S(1)} all-to-all(bf16[8,32,256]{2,1,0:T(8,128)(2,1)S(1)} %project.1), channel_id=1, replica_groups=mesh['ctx'=64,'tp'=8] {'tp'}, dimensions={0} | all-to-all | bytes 262144 | tf_op jit(solution)/shard_map/all_to_all | solution.py:290
  132.3 0.6 reduce_sum.12
  (1 shorter events, 0.0 us)
Async XLA Ops:
  0.7 37.5 %copy-start.1 = (s32[128]{0:T(128)S(1)}, s32[128]{0:T(128)}, u32[]{:S(2)}) copy-start(s32[128]{0:T(128)} %len_ref.1) | copy-start | bytes 1540
  2.0 17.5 %copy-start.3 = (bf16[1,2048,128]{2,1,0:T(8,128)(2,1)S(1)}, bf16[1,2048,128]{2,1,0:T(8,128)(2,1)}, u32[]{:S(2)}) copy-start(bf16[1,2048,128]{2,1,0:T(8,128)(2,1)} %get-tuple-element.37) | copy-start | bytes 1572868 | tf_op jit(solution)/shard_map/cond
  2.0 17.8 %copy-start.5 = (bf16[1,2048,128]{2,1,0:T(8,128)(2,1)S(1)}, bf16[1,2048,128]{2,1,0:T(8,128)(2,1)}, u32[]{:S(2)}) copy-start(bf16[1,2048,128]{2,1,0:T(8,128)(2,1)} %get-tuple-element.39) | copy-start | bytes 1572868 | tf_op jit(solution)/shard_map/cond
  2.0 17.8 %copy-start.7 = (f32[1,2048]{1,0:T(1,128)S(1)}, f32[1,2048]{1,0:T(1,128)}, u32[]{:S(2)}) copy-start(f32[1,2048]{1,0:T(1,128)} %get-tuple-element.40) | copy-start | bytes 24580 | tf_op jit(solution)/shard_map/cond
  2.0 36.2 %all-to-all-start.2 = ((bf16[64,64,128]{2,1,0:T(8,128)(2,1)}), bf16[64,64,128]{2,1,0:T(8,128)(2,1)}, u32[]{:S(2)}, u32[]{:S(2)}) async-start(bf16[64,64,128]{2,1,0:T(8,128)(2,1)} %broadcast_in_dim.13), calls=%async_computation.2 | async-start | bytes 2097152 | tf_op jit(solution)/shard_map/cond/branch_1_fun/all_to_all | solution.py:214
  19.8 0.7 copy-start.9
  82.8 25.3 %copy-start = (bf16[2048,256]{1,0:T(8,128)(2,1)S(1)}, bf16[2048,256]{1,0:T(8,128)(2,1)}, u32[]{:S(2)}) copy-start(bf16[2048,256]{1,0:T(8,128)(2,1)} %w_ref.1) | copy-start | bytes 3145732
